TPU v7x, 256 devices: a whole 4x4x8 slice. The times are simulated.
256 devices in a mesh: ifg: 16 (over z, core), strip: 16 (over y, x).
Axes of the slice: x: 4, y: 4, z: 8, core: 2. Of those that a mesh axis runs over, the one named last changes fastest.
Arguments:
- grad_x: float32 [64, 1024, 1024], P('ifg', 'strip'), may hold values from -3 to 3
- grad_y: float32 [64, 1024, 1024], P('ifg', 'strip'), may hold values from -3 to 3
- coherence: float32 [64, 1024, 1024], P('ifg', 'strip'), may hold values from 0 to 1, as said below
- pairs: int32 [64, 2], replicated, may hold values from 0 to 31, as said below
Outputs:
- unwrapped: float32 [64, 1024, 1024], P('ifg', 'strip')
- series: float32 [32, 1024, 1024], P('ifg', 'strip')
Inputs may be any that keep to these rules, and one draw needn't show every extreme that they name: Every row names an earlier date first and a later date second; the pairs connect all 32 dates. `coherence`: positive weights.
All inputs are finite; a program needn't handle non-finite values.
Results may differ from a plain program's by a relative error of at most 0.0003.
Values sent between devices are 32-bit elements; how exact they have to be, the bound alone decides.
A program may use at most 64 MiB of HBM per device.

v0:
```python
import jax
import jax.numpy as jnp
from jax import lax
from jax.sharding import PartitionSpec as P

DATES = 32
ITERS = 3


damping = 0.1


def extended(x, sides, width):
    for axis, dim in sides:
        size, length = (lax.axis_size(axis), x.shape[dim])
        up = [(i, (i + 1) % size) for i in range(size - 1)]
        down = [(j, i) for i, j in up]
        last = lax.slice_in_dim(x, length - width, length, axis=dim)
        initial = lax.slice_in_dim(x, 0, width, axis=dim)
        before = lax.ppermute(last, axis, up)
        after = lax.ppermute(initial, axis, down)
        x = jnp.concatenate([before, x, after], axis=dim)
    return x


def prev_col(field):
    return jnp.pad(field, ((0, 0), (0, 0), (1, 0)))[:, :, :-1]


def inverse_map(pairs):
    slots = jnp.arange(DATES, dtype=jnp.int32)
    design = (pairs[:, 1:2] == slots[None, :]).astype(jnp.float32) - (
        pairs[:, 0:1] == slots[None, :]
    ).astype(jnp.float32)
    normal = jnp.dot(design.T, design, precision=lax.Precision.HIGHEST) + 1.0
    factor = jnp.linalg.cholesky(normal)
    return jax.scipy.linalg.cho_solve((factor, True), design.T)


def operate(field, wx, wy_ext):
    padded = extended(field, (("strip", 1),), 1)
    diff_y = padded[:, 1:, :] - padded[:, :-1, :]
    flux_y = wy_ext * diff_y
    diff_x = jnp.pad(field[:, :, 1:] - field[:, :, :-1], ((0, 0), (0, 0), (0, 1)))
    flux_x = wx * diff_x
    return damping * field - (flux_x - prev_col(flux_x) + flux_y[:, 1:, :] - flux_y[:, :-1, :])


def squares(residual):
    return lax.psum(jnp.sum(residual * residual, axis=(1, 2)), "strip")


def on_device(grad_x, grad_y, coherence, pairs):
    stacked = jnp.stack([coherence, grad_y])
    padded = extended(stacked, (("strip", 2),), 1)
    weight_ext = padded[0]
    grad_y_ext = padded[1]
    wy_ext = weight_ext[:, :-1, :] * weight_ext[:, 1:, :]
    flux_y = wy_ext * grad_y_ext[:, :-1, :]
    wx = jnp.pad(coherence[:, :, :-1] * coherence[:, :, 1:], ((0, 0), (0, 0), (0, 1)))
    flux_x = wx * grad_x
    rhs = -(flux_x - prev_col(flux_x) + flux_y[:, 1:, :] - flux_y[:, :-1, :])
    solution = jnp.zeros_like(rhs)
    residual = rhs
    direction = rhs
    norm_now = squares(residual)
    for step in range(ITERS):
        image = operate(direction, wx, wy_ext)
        curve = lax.psum(jnp.sum(direction * image, axis=(1, 2)), "strip")
        alpha = norm_now / curve
        solution = solution + alpha[:, None, None] * direction
        residual = residual - alpha[:, None, None] * image
        norm_next = squares(residual)
        direction = residual + (norm_next / norm_now)[:, None, None] * direction
        norm_now = norm_next
    mapping = inverse_map(pairs)
    local = jnp.einsum(
        "dk,krc->drc",
        mapping,
        lax.all_to_all(solution, "ifg", split_axis=2, concat_axis=0, tiled=True),
        precision=lax.Precision.HIGHEST,
    )
    series = lax.all_to_all(local, "ifg", split_axis=0, concat_axis=2, tiled=True)
    return (solution, series)


def solution(mesh):
    in_specs = (P("ifg", "strip", None), P("ifg", "strip", None), P("ifg", "strip", None), P())
    out_specs = (P("ifg", "strip", None), P("ifg", "strip", None))
    return jax.shard_map(
        on_device, mesh=mesh, in_specs=in_specs, out_specs=out_specs, check_vma=False
    )
```

profile of v0, /device:TPU:1, one launch (start us, length us, event | category | flops | bytes accessed | tf_op | source)
XLA Modules:
  0.0 322.9 jit_solution(10777862098146449319)
XLA Ops:
  0.6 2.0 copy.69
  2.6 0.7 copy.68
  3.4 3.9 %collective-permute-start = (f32[2,4,1,1024]{3,1,2,0:T(4,128)S(1)}, f32[2,4,1,1024]{3,1,2,0:T(4,128)S(1)}, u32[]{:S(2)}, u32[]{:S(2)}) collective-permute-start(f32[2,4,1,1024]{3,1,2,0:T(4,128)S(1)} %get-tuple-element.23), channel_id=1, source_target_pairs={{0,1},{1,2},{2,3},{3,4},{4,5},{5,6},{6,7},{7,8},{8,9},{9,10},{10,1... | collective-permute-start | bytes 98312 | tf_op jit(solution)/shard_map/ppermute | solution.py:20
  7.3 1.4 collective-permute-start.1
  8.7 0.6 slice_multiply_fusion.2
  9.4 0.8 copy_multiply_fusion
  10.2 1.9 collective-permute-done.1
  12.1 0.5 pad_maximum_fusion
  12.7 0.4 slice_bitcast_fusion.1
  13.1 0.5 slice_multiply_fusion
  13.6 0.8 fusion.31
  14.5 0.6 slice_subtract_fusion.2
  15.1 1.3 collective-permute-start.2
  16.4 4.0 %collective-permute-start.3 = (f32[4,1,1024]{2,0,1:T(4,128)S(1)}, f32[4,1,1024]{2,0,1:T(4,128)S(1)}, u32[]{:S(2)}, u32[]{:S(2)}) collective-permute-start(f32[4,1,1024]{2,0,1:T(4,128)S(1)} %get-tuple-element.29), channel_id=1, source_target_pairs={{0,1},{1,2},{2,3},{3,4},{4,5},{5,6},{6,7},{7,8},{8,9},{9,10},{10,1... | collective-permute-start | bytes 49160 | tf_op jit(solution)/shard_map/ppermute | solution.py:20
  20.4 0.4 pad_multiply_fusion.2
  20.8 0.4 collective-permute-done.3
  21.2 0.5 fusion
  21.7 1.2 multiply_reduce_fusion.3
  22.9 34.1 %all-reduce.8 = (f32[4]{0:T(128)S(1)}, f32[4]{0:T(128)S(1)}) all-reduce(f32[4]{0:T(128)S(1)} %get-tuple-element.9, f32[4]{0:T(128)S(1)} %get-tuple-element.8), channel_id=1, replica_groups=mesh['ifg'=16,'strip'=16] {'strip'}, use_global_device_ids=true, to_apply=%region_1.2 | all-reduce | flops 8 | bytes 64 | tf_op jit(solution)/shard_map/psum | solution.py:50
  57.0 1.7 multiply_reduce_fusion.2
  58.7 28.7 %psum.44 = f32[4]{0:T(128)S(1)} all-reduce(f32[4]{0:T(128)S(1)} %get-tuple-element.14), channel_id=1, replica_groups=mesh['ifg'=16,'strip'=16] {'strip'}, use_global_device_ids=true, to_apply=%region_5.6 | all-reduce | flops 4 | bytes 32 | tf_op jit(solution)/shard_map/psum | solution.py:50
  87.4 1.7 multiply_add_fusion.2
  89.1 0.6 slice_subtract_fusion.1
  89.7 1.3 collective-permute-start.4
  91.0 4.6 %collective-permute-start.5 = (f32[4,1,1024]{2,0,1:T(4,128)S(1)}, f32[4,1,1024]{2,0,1:T(4,128)S(1)}, u32[]{:S(2)}, u32[]{:S(2)}) collective-permute-start(f32[4,1,1024]{2,0,1:T(4,128)S(1)} %get-tuple-element.27), channel_id=1, source_target_pairs={{0,1},{1,2},{2,3},{3,4},{4,5},{5,6},{6,7},{7,8},{8,9},{9,10},{10,1... | collective-permute-start | bytes 49160 | tf_op jit(solution)/shard_map/ppermute | solution.py:20
  95.6 0.4 pad_multiply_fusion.1
  96.3 0.5 fusion.1
  96.8 2.2 multiply_reduce_fusion.1
  99.0 30.2 %psum.45 = f32[4]{0:T(128)S(1)} all-reduce(f32[4]{0:T(128)S(1)} %get-tuple-element.12), channel_id=1, replica_groups=mesh['ifg'=16,'strip'=16] {'strip'}, use_global_device_ids=true, to_apply=%region_7.8 | all-reduce | flops 4 | bytes 32 | tf_op jit(solution)/shard_map/psum | solution.py:69
  129.2 2.0 multiply_reduce_fusion
  131.1 28.5 %psum.46 = f32[4]{0:T(128)S(1)} all-reduce(f32[4]{0:T(128)S(1)} %multiply_reduce_fusion), channel_id=1, replica_groups=mesh['ifg'=16,'strip'=16] {'strip'}, use_global_device_ids=true, to_apply=%region_9.10 | all-reduce | flops 4 | bytes 32 | tf_op jit(solution)/shard_map/psum | solution.py:50
  159.6 2.3 multiply_add_fusion.1
  161.9 0.6 slice_subtract_fusion
  162.6 1.3 collective-permute-start.6
  163.9 4.3 %collective-permute-start.7 = (f32[4,1,1024]{2,0,1:T(4,128)S(1)}, f32[4,1,1024]{2,0,1:T(4,128)S(1)}, u32[]{:S(2)}, u32[]{:S(2)}) collective-permute-start(f32[4,1,1024]{2,0,1:T(4,128)S(1)} %get-tuple-element.25), channel_id=1, source_target_pairs={{0,1},{1,2},{2,3},{3,4},{4,5},{5,6},{6,7},{7,8},{8,9},{9,10},{10,1... | collective-permute-start | bytes 49160 | tf_op jit(solution)/shard_map/ppermute | solution.py:20
  168.2 0.4 pad_multiply_fusion
  168.6 0.4 collective-permute-done.7
  169.1 0.5 fusion.2
  169.6 1.2 fusion.19
  170.8 30.6 %psum.47 = f32[4]{0:T(128)S(1)} all-reduce(f32[4]{0:T(128)S(1)} %fusion.19), channel_id=1, replica_groups=mesh['ifg'=16,'strip'=16] {'strip'}, use_global_device_ids=true, to_apply=%region_11.12 | all-reduce | flops 4 | bytes 32 | tf_op jit(solution)/shard_map/psum | solution.py:69
  201.4 1.7 multiply_add_fusion
  203.1 1.9 copy.58
  205.0 2.9 reshape.23
  207.9 49.5 %all-to-all-start = ((f32[16,1,16384]{2,1,0:T(1,128)}), f32[16,1,16384]{2,1,0:T(1,128)S(1)}, u32[]{:S(2)}, u32[]{:S(2)}) async-start(f32[16,1,16384]{2,1,0:T(1,128)} %reshape.23), calls=%async_computation | async-start | bytes 2097152 | tf_op jit(solution)/shard_map/all_to_all | solution.py:80
  257.4 0.3 convolution_add_fusion
  257.8 2.9 cholesky.16
  260.7 0.6 compare_reduce_fusion
  261.3 0.7 fusion.21
  262.0 2.4 custom-call.10
  264.9 20.4 %all-to-all-done = f32[16,1,16384]{2,1,0:T(1,128)S(1)} async-done(((f32[16,1,16384]{2,1,0:T(1,128)}), f32[16,1,16384]{2,1,0:T(1,128)S(1)}, u32[]{:S(2)}, u32[]{:S(2)}) %all-to-all-start) | async-done | bytes 1048608 | tf_op jit(solution)/shard_map/all_to_all | solution.py:80
  285.3 0.5 broadcast.104
  285.8 3.1 reduce.6
  288.9 2.8 reshape.24
  291.7 3.1 copy.59
  294.8 1.1 fusion.37
  295.9 0.6 copy.60
  296.6 1.4 reshape.25
  298.0 3.5 %all-to-all-start.1 = ((f32[16,1,8192]{2,1,0:T(1,128)}), f32[16,1,8192]{2,1,0:T(1,128)S(1)}, u32[]{:S(2)}, u32[]{:S(2)}) async-start(f32[16,1,8192]{2,1,0:T(1,128)} %reshape.25), calls=%async_computation.1 | async-start | bytes 1048576 | tf_op jit(solution)/shard_map/all_to_all | solution.py:83
  301.5 1.6 copy.62
  303.1 15.7 %all-to-all-done.1 = f32[16,1,8192]{2,1,0:T(1,128)S(1)} async-done(((f32[16,1,8192]{2,1,0:T(1,128)}), f32[16,1,8192]{2,1,0:T(1,128)S(1)}, u32[]{:S(2)}, u32[]{:S(2)}) %all-to-all-start.1) | async-done | bytes 524320 | tf_op jit(solution)/shard_map/all_to_all | solution.py:83
  318.8 1.9 reduce.7
  320.7 0.4 reshape.26
  321.1 0.6 copy.61
  321.7 1.1 all_to_all.33
  (40 shorter events, 0.9 us)
Async XLA Ops:
  0.6 2.0 copy-start.8
  3.4 6.9 %collective-permute-start = (f32[2,4,1,1024]{3,1,2,0:T(4,128)S(1)}, f32[2,4,1,1024]{3,1,2,0:T(4,128)S(1)}, u32[]{:S(2)}, u32[]{:S(2)}) collective-permute-start(f32[2,4,1,1024]{3,1,2,0:T(4,128)S(1)} %get-tuple-element.23), channel_id=1, source_target_pairs={{0,1},{1,2},{2,3},{3,4},{4,5},{5,6},{6,7},{7,8},{8,9},{9,10},{10,1... | collective-permute-start | bytes 98312 | tf_op jit(solution)/shard_map/ppermute | solution.py:20
  7.3 2.1 copy-start.7
  7.3 4.8 %collective-permute-start.1 = (f32[2,4,1,1024]{3,1,2,0:T(4,128)S(1)}, f32[2,4,1,1024]{3,1,2,0:T(4,128)S(1)}, u32[]{:S(2)}, u32[]{:S(2)}) collective-permute-start(f32[2,4,1,1024]{3,1,2,0:T(4,128)S(1)} %get-tuple-element.24), channel_id=1, source_target_pairs={{1,0},{2,1},{3,2},{4,3},{5,4},{6,5},{7,6},{8,7},{9,8},{10,9},{11,1... | collective-permute-start | bytes 98312 | tf_op jit(solution)/shard_map/ppermute | solution.py:21
  13.6 7.6 %copy-start.2 = (f32[4,65,1024]{2,0,1:T(4,128)}, f32[4,65,1024]{2,0,1:T(4,128)S(1)}, u32[]{:S(2)}) copy-start(f32[4,65,1024]{2,0,1:T(4,128)S(1)} %get-tuple-element.20) | copy-start | bytes 3194884
  14.4 72.9 %copy-start = (f32[4,64,1024]{2,0,1:T(4,128)}, f32[4,64,1024]{2,0,1:T(4,128)S(1)}, u32[]{:S(2)}) copy-start(f32[4,64,1024]{2,0,1:T(4,128)S(1)} %get-tuple-element.18) | copy-start | bytes 3145732
  15.1 5.7 %collective-permute-start.2 = (f32[4,1,1024]{2,0,1:T(4,128)S(1)}, f32[4,1,1024]{2,0,1:T(4,128)S(1)}, u32[]{:S(2)}, u32[]{:S(2)}) collective-permute-start(f32[4,1,1024]{2,0,1:T(4,128)S(1)} %get-tuple-element.30), channel_id=1, source_target_pairs={{1,0},{2,1},{3,2},{4,3},{5,4},{6,5},{7,6},{8,7},{9,8},{10,9},{11,1... | collective-permute-start | bytes 49160 | tf_op jit(solution)/shard_map/ppermute | solution.py:21
  16.4 4.8 %collective-permute-start.3 = (f32[4,1,1024]{2,0,1:T(4,128)S(1)}, f32[4,1,1024]{2,0,1:T(4,128)S(1)}, u32[]{:S(2)}, u32[]{:S(2)}) collective-permute-start(f32[4,1,1024]{2,0,1:T(4,128)S(1)} %get-tuple-element.29), channel_id=1, source_target_pairs={{0,1},{1,2},{2,3},{3,4},{4,5},{5,6},{6,7},{7,8},{8,9},{9,10},{10,1... | collective-permute-start | bytes 49160 | tf_op jit(solution)/shard_map/ppermute | solution.py:20
  89.7 6.3 %collective-permute-start.4 = (f32[4,1,1024]{2,0,1:T(4,128)S(1)}, f32[4,1,1024]{2,0,1:T(4,128)S(1)}, u32[]{:S(2)}, u32[]{:S(2)}) collective-permute-start(f32[4,1,1024]{2,0,1:T(4,128)S(1)} %get-tuple-element.28), channel_id=1, source_target_pairs={{1,0},{2,1},{3,2},{4,3},{5,4},{6,5},{7,6},{8,7},{9,8},{10,9},{11,1... | collective-permute-start | bytes 49160 | tf_op jit(solution)/shard_map/ppermute | solution.py:21
  91.0 5.3 %copy-start.3 = (f32[4,65,1024]{2,0,1:T(4,128)S(1)}, f32[4,65,1024]{2,0,1:T(4,128)}, u32[]{:S(2)}) copy-start(f32[4,65,1024]{2,0,1:T(4,128)} %copy-done.2) | copy-start | bytes 3194884
  91.0 5.2 %collective-permute-start.5 = (f32[4,1,1024]{2,0,1:T(4,128)S(1)}, f32[4,1,1024]{2,0,1:T(4,128)S(1)}, u32[]{:S(2)}, u32[]{:S(2)}) collective-permute-start(f32[4,1,1024]{2,0,1:T(4,128)S(1)} %get-tuple-element.27), channel_id=1, source_target_pairs={{0,1},{1,2},{2,3},{3,4},{4,5},{5,6},{6,7},{7,8},{8,9},{9,10},{10,1... | collective-permute-start | bytes 49160 | tf_op jit(solution)/shard_map/ppermute | solution.py:20
  96.8 32.4 %copy-start.5 = (f32[4,64,1024]{2,0,1:T(4,128)S(1)}, f32[4,64,1024]{2,0,1:T(4,128)}, u32[]{:S(2)}) copy-start(f32[4,64,1024]{2,0,1:T(4,128)} %get-tuple-element.15) | copy-start | bytes 3145732
  162.6 6.1 %collective-permute-start.6 = (f32[4,1,1024]{2,0,1:T(4,128)S(1)}, f32[4,1,1024]{2,0,1:T(4,128)S(1)}, u32[]{:S(2)}, u32[]{:S(2)}) collective-permute-start(f32[4,1,1024]{2,0,1:T(4,128)S(1)} %get-tuple-element.26), channel_id=1, source_target_pairs={{1,0},{2,1},{3,2},{4,3},{5,4},{6,5},{7,6},{8,7},{9,8},{10,9},{11,1... | collective-permute-start | bytes 49160 | tf_op jit(solution)/shard_map/ppermute | solution.py:21
  163.9 5.2 %copy-start.4 = (f32[4,65,1024]{2,0,1:T(4,128)S(1)}, f32[4,65,1024]{2,0,1:T(4,128)}, u32[]{:S(2)}) copy-start(f32[4,65,1024]{2,0,1:T(4,128)} %copy-done.2) | copy-start | bytes 3194884
  163.9 5.2 %collective-permute-start.7 = (f32[4,1,1024]{2,0,1:T(4,128)S(1)}, f32[4,1,1024]{2,0,1:T(4,128)S(1)}, u32[]{:S(2)}, u32[]{:S(2)}) collective-permute-start(f32[4,1,1024]{2,0,1:T(4,128)S(1)} %get-tuple-element.25), channel_id=1, source_target_pairs={{0,1},{1,2},{2,3},{3,4},{4,5},{5,6},{6,7},{7,8},{8,9},{9,10},{10,1... | collective-permute-start | bytes 49160 | tf_op jit(solution)/shard_map/ppermute | solution.py:20
  169.6 31.8 %copy-start.1 = (f32[4,64,1024]{2,0,1:T(4,128)S(1)}, f32[4,64,1024]{2,0,1:T(4,128)}, u32[]{:S(2)}) copy-start(f32[4,64,1024]{2,0,1:T(4,128)} %copy-done) | copy-start | bytes 3145732
  207.9 49.5 %copy-start.9 = (s32[64,2]{0,1:T(2,128)S(1)}, s32[64,2]{0,1:T(2,128)}, u32[]{:S(2)}) copy-start(s32[64,2]{0,1:T(2,128)} %param.7) | copy-start | bytes 1540
  207.9 77.4 %all-to-all-start = ((f32[16,1,16384]{2,1,0:T(1,128)}), f32[16,1,16384]{2,1,0:T(1,128)S(1)}, u32[]{:S(2)}, u32[]{:S(2)}) async-start(f32[16,1,16384]{2,1,0:T(1,128)} %reshape.23), calls=%async_computation | async-start | bytes 2097152 | tf_op jit(solution)/shard_map/all_to_all | solution.py:80
  296.5 5.0 %copy-start.6 = (f32[4,64,1024]{2,0,1:T(4,128)S(1)}, f32[4,64,1024]{2,0,1:T(4,128)}, u32[]{:S(2)}) copy-start(f32[4,64,1024]{2,0,1:T(4,128)} %multiply_add_fusion) | copy-start | bytes 3145732
  298.0 20.8 %all-to-all-start.1 = ((f32[16,1,8192]{2,1,0:T(1,128)}), f32[16,1,8192]{2,1,0:T(1,128)S(1)}, u32[]{:S(2)}, u32[]{:S(2)}) async-start(f32[16,1,8192]{2,1,0:T(1,128)} %reshape.25), calls=%async_computation.1 | async-start | bytes 1048576 | tf_op jit(solution)/shard_map/all_to_all | solution.py:83
where the time goes:
time: 324 us; the launch traced here: 323 us
  blocking collectives  152 us (47%)
  starting transfers between devices  75.1 us (23%)
  waiting for transfers between devices  39.1 us (12%)
  other arithmetic  33.5 us (10%)
  local copies, waits for them, and re-layouts  20.2 us (6%)
    psum x3, blocking collectives, squares(): return lax.psum(jnp.sum(residual * residual, axis=(1, 2)), 'strip')  91.3 us
    psum x2, blocking collectives, on_device(): curve = lax.psum(jnp.sum(direction * image, axis=(1, 2)), 'strip')  60.8 us
    all_to_all x1, starting transfers between devices, on_device(): lax.all_to_all(solution, 'ifg', split_axis=2, concat_axis=0, tiled=True)  49.5 us
    all_to_all x1, waiting for transfers between devices, on_device(): lax.all_to_all(solution, 'ifg', split_axis=2, concat_axis=0, tiled=True)  20.4 us
    ppermute x4, starting transfers between devices, extended(): before = lax.ppermute(last, axis, up)  16.8 us
    all_to_all x1, waiting for transfers between devices, on_device(): lax.all_to_all(local, 'ifg', split_axis=0, concat_axis=2, tiled=True)  15.7 us
    unnamed x27, local copies, waits for them, and re-layouts  11.8 us
  transfers between devices with their start and end apart: 10, of which 6 were waited for; matrix products, arithmetic and copies ran while one was open for 4% of the time, Pallas kernels for 0%

commit v1 on v0

v1 whole, which is shorter than its diff:
```python
import jax
import jax.numpy as jnp
from jax import lax
from jax.experimental import pallas as pl
from jax.experimental.pallas import tpu as pltpu
from jax.sharding import PartitionSpec as P

MESH = pl.DeviceIdType.MESH
DAMPING = 0.1
DATES = 32
IFGS = 64
GROUPS = 16
STRIPS = 16
K = 4
OWN = 2
ROWS = 64
COLS = 1024
TILES = ROWS // 8
CHUNKS = 4
EPS = 3e-7


def tile(t):
    return slice(8 * t, 8 * t + 8)


def rows_iota():
    return lax.broadcasted_iota(jnp.int32, (8, COLS), 0)


def fold(field):
    total = field[:, :128]
    for c in range(1, COLS // 128):
        total = total + field[:, 128 * c : 128 * c + 128]
    return total


def next_row(now, after):
    return jnp.where(rows_iota() == 7, pltpu.roll(after, 7, 0), pltpu.roll(now, 7, 0))


def edge_x(coherence):
    lanes = lax.broadcasted_iota(jnp.int32, (8, COLS), 1)
    return jnp.where(lanes == COLS - 1, 0.0, coherence * pltpu.roll(coherence, COLS - 1, 1))


def laplace(p_ref, q_ref, wx_ref, wy_ref, i, first, last, inner):
    top = rows_iota() == 0
    now = p_ref[i, tile(first), :]
    if first > 0:
        before = p_ref[i, tile(first - 1), :]
        carry = pltpu.roll(wy_ref[i, tile(first - 1), :] * (next_row(before, now) - before), 1, 0)
    else:
        carry = jnp.zeros((8, COLS), jnp.float32)
    for t in range(first, last + 1):
        after = p_ref[i, tile(t + 1), :] if t < TILES + 1 else now
        flux_y = wy_ref[i, tile(t), :] * (next_row(now, after) - now)
        flux_x = wx_ref[i, tile(t), :] * (pltpu.roll(now, COLS - 1, 1) - now)
        turned = pltpu.roll(flux_y, 1, 0)
        out = pltpu.roll(flux_x, 1, 1) - flux_x + jnp.where(top, carry, turned) - flux_y
        q_ref[i, tile(t), :] = out
        inner(t, now, out)
        carry = turned
        now = after


def energy(p_ref, wx_ref, wy_ref, i, tiles):
    total = jnp.zeros((8, 128), jnp.float32)
    for t in tiles:
        now = p_ref[i, tile(t), :]
        diff_y = next_row(now, p_ref[i, tile(t + 1), :]) - now
        diff_x = pltpu.roll(now, COLS - 1, 1) - now
        total = total + fold(
            wy_ref[i, tile(t), :] * diff_y * diff_y + wx_ref[i, tile(t), :] * diff_x * diff_x
        )
    return total


def coefficients(m):
    a = [m[j + 1] + DAMPING * m[j] for j in range(5)]
    zero = jnp.zeros_like(m[0])
    d0 = a[0]
    good0 = d0 > 0.0
    inv0 = 1.0 / jnp.where(good0, d0, 1.0)
    l1 = a[1] * inv0
    l2 = a[2] * inv0
    d1 = a[2] - l1 * a[1]
    good1 = d1 > EPS * a[2]
    inv1 = jnp.where(good1, 1.0 / jnp.where(good1, d1, 1.0), zero)
    l3 = (a[3] - l2 * a[1]) * inv1
    d2 = a[4] - l2 * a[2] - l3 * (a[3] - l2 * a[1])
    good2 = good1 & (d2 > EPS * a[4])
    inv2 = jnp.where(good2, 1.0 / jnp.where(good2, d2, 1.0), zero)
    y1 = m[1] - l1 * m[0]
    y2 = m[2] - l2 * m[0] - l3 * y1
    c2 = y2 * inv2
    c1 = y1 * inv1 - l3 * c2
    c0 = m[0] * inv0 - l1 * c1 - l2 * c2
    return c0, c1, c2


def inverse_rows(pairs):
    lanes = lax.broadcasted_iota(jnp.int32, (IFGS, 128), 1)
    rows = lax.broadcasted_iota(jnp.int32, (IFGS, 128), 0)
    design = (pairs[:, 1:2] == lanes).astype(jnp.float32) - (pairs[:, 0:1] == lanes).astype(
        jnp.float32
    )
    both = design + (lanes - DATES == rows).astype(jnp.float32)
    table = lax.dot_general(
        design, both, (((0,), (0,)), ((), ())), precision=lax.Precision.HIGHEST,
        preferred_element_type=jnp.float32,
    )[:DATES]
    spread = lax.broadcasted_iota(jnp.int32, (DATES, 128), 1)
    level = lax.broadcasted_iota(jnp.int32, (DATES, 1), 0)
    table = table + (spread < DATES).astype(jnp.float32)
    for j in range(DATES):
        row = table[j : j + 1, :] / table[j : j + 1, j : j + 1]
        column = table[:, j : j + 1] - (level == j).astype(jnp.float32)
        table = table - column * row
    return table


def kernel(
    gx_hbm, gy_hbm, co_hbm, pairs_ref, x_hbm, series_hbm,
    gx, gy, co, wx, wy, v0, v1, v2, x, sums, moments, folded, coef, spread, phases, dates,
    load_sem, halo_send, halo_recv, sum_send, sum_recv, x_send, x_recv, s_send, s_recv, out_sem,
):
    g, s = lax.axis_index("ifg"), lax.axis_index("strip")
    z, core = g // 2, lax.rem(g, 2)
    rows = rows_iota()

    loads = []
    for i in range(K):
        for a, (src, dst, low) in enumerate(((co_hbm, co, 8), (gy_hbm, gy, 8), (gx_hbm, gx, 0))):
            loads.append(
                pltpu.make_async_copy(src.at[i], dst.at[i, low : low + ROWS], load_sem.at[i, a])
            )
    for copy in loads:
        copy.start()

    barrier = pltpu.get_barrier_semaphore()

    @pl.loop(1, STRIPS)
    def _(d):
        pl.semaphore_signal(
            barrier, inc=1, device_id=(g, lax.rem(s + d, STRIPS)), device_id_type=MESH
        )
        pl.semaphore_signal(
            barrier, inc=1, device_id=(lax.rem(g + d, GROUPS), s), device_id_type=MESH
        )

    nothing = jnp.zeros((K, 8, COLS), jnp.float32)

    @pl.when(s == 0)
    def _():
        co[:, tile(0), :] = nothing
        gy[:, tile(0), :] = nothing
        v0[:, tile(0), :] = nothing

    @pl.when(s == STRIPS - 1)
    def _():
        co[:, tile(TILES + 1), :] = nothing
        v0[:, tile(TILES + 1), :] = nothing

    for copy in loads:
        copy.wait()

    @pl.loop(0, K)
    def _(i):
        carry = jnp.zeros((8, COLS), jnp.float32)
        now = co[i, tile(1), :]
        for t in range(1, TILES + 1):
            after = co[i, tile(t + 1), :] if t < TILES else jnp.zeros((8, COLS), jnp.float32)
            weight_x = edge_x(now)
            weight_y = now * next_row(now, after)
            flux_x = weight_x * gx[i, tile(t - 1), :]
            flux_y = weight_y * gy[i, tile(t), :]
            turned = pltpu.roll(flux_y, 1, 0)
            wx[i, tile(t), :] = weight_x
            wy[i, tile(t), :] = weight_y
            v0[i, tile(t), :] = (
                pltpu.roll(flux_x, 1, 1) - flux_x + jnp.where(rows == 0, carry, turned) - flux_y
            )
            carry = turned
            now = after

    pl.semaphore_wait(barrier, STRIPS + GROUPS - 2)

    def halo(n, src, dst, low, high, shift, device):
        return pltpu.make_async_remote_copy(
            src_ref=src.at[:, low:high],
            dst_ref=dst.at[:, low + shift : high + shift],
            send_sem=halo_send.at[n],
            recv_sem=halo_recv.at[n],
            device_id=(g, device),
            device_id_type=MESH,
        )

    up = jnp.maximum(s - 1, 0)
    down = jnp.minimum(s + 1, STRIPS - 1)
    upward = [halo(0, co, co, 8, 11, ROWS, up), halo(1, v0, v0, 8, 11, ROWS, up)]
    downward = [
        halo(2, co, co, 6 + ROWS, 8 + ROWS, -ROWS, down),
        halo(3, v0, v0, 6 + ROWS, 8 + ROWS, -ROWS, down),
        halo(4, gy, gy, 7 + ROWS, 8 + ROWS, -ROWS, down),
    ]

    @pl.when(s > 0)
    def _():
        for copy in upward:
            copy.start()

    @pl.when(s < STRIPS - 1)
    def _():
        for copy in downward:
            copy.start()

    def first_pass(i, spans):
        totals = [jnp.zeros((8, 128), jnp.float32)] * 3

        def inner(t, p, q):
            if 1 <= t <= TILES:
                for n, product in enumerate((p * p, p * q, q * q)):
                    totals[n] = totals[n] + fold(product)

        for low, high in spans:
            laplace(v0, v1, wx, wy, i, low, high, inner)
        return totals

    def second_pass(i, spans):
        totals = [jnp.zeros((8, 128), jnp.float32)] * 2

        def inner(t, p, q):
            if 1 <= t <= TILES:
                for n, product in enumerate((p * q, q * q)):
                    totals[n] = totals[n] + fold(product)

        for low, high in spans:
            laplace(v1, v2, wx, wy, i, low, high, inner)
        return totals

    @pl.loop(0, K)
    def _(i):
        totals = first_pass(i, [(2, 7)]) + second_pass(i, [(3, 6)])
        totals.append(energy(v2, wx, wy, i, range(3, 6)))
        for n, total in enumerate(totals):
            sums[i, n] = total

    @pl.when(s > 0)
    def _():
        for copy in upward:
            copy.wait_send()
        for copy in downward:
            copy.wait_recv()

    @pl.when(s < STRIPS - 1)
    def _():
        for copy in downward:
            copy.wait_send()
        for copy in upward:
            copy.wait_recv()

    for i in range(K):
        low, high, beyond = co[i, tile(0), :], co[i, tile(TILES), :], co[i, tile(TILES + 1), :]
        wx[i, tile(0), :] = edge_x(low)
        wx[i, tile(TILES + 1), :] = edge_x(beyond)
        weight_low = low * next_row(low, co[i, tile(1), :])
        weight_high = high * next_row(high, beyond)
        wy[i, tile(0), :] = weight_low
        wy[i, tile(TILES), :] = weight_high
        wy[i, tile(TILES + 1), :] = beyond * next_row(beyond, beyond)
        for t, weight in ((0, weight_low), (TILES, weight_high)):
            flux = weight * gy[i, tile(t), :]
            here, there = v0[i, tile(t), :], v0[i, tile(t + 1), :]
            v0[i, tile(t), :] = jnp.where(rows == 7, here - flux, here)
            v0[i, tile(t + 1), :] = jnp.where(rows == 0, there + pltpu.roll(flux, 1, 0), there)

    @pl.loop(0, K)
    def _(i):
        totals = first_pass(i, [(0, 1), (8, 9)]) + second_pass(i, [(1, 2), (7, 9)])
        totals.append(energy(v2, wx, wy, i, (1, 2, 6, 7, 8)))
        for n, total in enumerate(totals):
            moments[s, pl.ds(K * n + i, 1), :] = jnp.sum(sums[i, n] + total, axis=0, keepdims=True)

    def share(d):
        return pltpu.make_async_remote_copy(
            src_ref=moments.at[s],
            dst_ref=moments.at[s],
            send_sem=sum_send,
            recv_sem=sum_recv,
            device_id=(g, lax.rem(s + d, STRIPS)),
            device_id_type=MESH,
        )

    @pl.loop(1, STRIPS)
    def _(d):
        share(d).start()

    table = inverse_rows(pairs_ref[...])
    for k in range(IFGS):
        spread[k] = jnp.broadcast_to(table[:, DATES + k : DATES + k + 1], (DATES, 128))

    others = moments.at[0 : STRIPS - 1]
    pltpu.make_async_copy(others, others, sum_recv).wait()
    total = moments[0]
    for d in range(1, STRIPS):
        total = total + moments[d]
    folded[...] = jnp.broadcast_to(jnp.sum(total, axis=1, keepdims=True), folded.shape)
    for j, c in enumerate(coefficients([folded[K * n : K * n + K, :] for n in range(6)])):
        coef[j] = c

    def send_x(d, q):
        t = lax.rem(g + d, GROUPS)
        row = pl.multiple_of(32 * lax.rem(t, 2) + 8 * q, 8)
        column = pl.multiple_of(128 * (t // 2), 128)
        return pltpu.make_async_remote_copy(
            src_ref=x.at[:, pl.ds(row, 8), pl.ds(column, 128)],
            dst_ref=phases.at[pl.ds(K * g, K), pl.ds(8 * q, 8)],
            send_sem=x_send.at[q],
            recv_sem=x_recv.at[q],
            device_id=(t, s),
            device_id_type=MESH,
        )

    own_column = pl.multiple_of(128 * z, 128)
    for q in range(CHUNKS):

        @pl.loop(0, K)
        def _(i):
            c0, c1, c2 = (coef[j, pl.ds(i, 1), 0:1] for j in range(3))
            for half in range(2):
                t = 4 * half + q
                x[i, tile(t), :] = (
                    c0 * v0[i, tile(t + 1), :] + c1 * v1[i, tile(t + 1), :] + c2 * v2[i, tile(t + 1), :]
                )

        @pl.loop(1, GROUPS)
        def _(d):
            send_x(d, q).start()

        own_row = pl.multiple_of(32 * core + 8 * q, 8)
        phases[pl.ds(K * g, K), tile(q), :] = x[:, pl.ds(own_row, 8), pl.ds(own_column, 128)]

    x_out = pltpu.make_async_copy(x, x_hbm, out_sem.at[CHUNKS])
    x_out.start()

    def place(q):
        row = pl.multiple_of(32 * core + 8 * q, 8)
        return series_hbm.at[:, pl.ds(row, 8), pl.ds(own_column, 128)]

    def send_s(d, q):
        t = lax.rem(g + d, GROUPS)
        return pltpu.make_async_remote_copy(
            src_ref=dates.at[pl.ds(OWN * t, OWN), tile(q)],
            dst_ref=place(q),
            send_sem=s_send.at[q],
            recv_sem=s_recv.at[q],
            device_id=(t, s),
            device_id_type=MESH,
        )

    own = []
    for q in range(CHUNKS):
        others = phases.at[0 : K * (GROUPS - 1), tile(q)]
        pltpu.make_async_copy(others, others, x_recv.at[q]).wait()

        def add(k, totals):
            phase = phases[k, tile(q), :]
            return tuple(
                total + spread[k, d : d + 1, :] * phase for d, total in enumerate(totals)
            )

        totals = lax.fori_loop(0, IFGS, add, (jnp.zeros((8, 128), jnp.float32),) * DATES)
        for d in range(DATES):
            dates[d, tile(q), :] = totals[d]

        @pl.loop(1, GROUPS)
        def _(d):
            send_s(d, q).start()

        own.append(pltpu.make_async_copy(dates.at[pl.ds(OWN * g, OWN), tile(q)], place(q), out_sem.at[q]))
        own[q].start()

    pltpu.make_async_copy(moments.at[0 : STRIPS - 1], moments.at[0 : STRIPS - 1], sum_send).wait()
    for q in range(CHUNKS):
        others = phases.at[0 : K * (GROUPS - 1), tile(q)]
        pltpu.make_async_copy(others, others, x_send.at[q]).wait()
        others = dates.at[0 : OWN * (GROUPS - 1), tile(q)]
        pltpu.make_async_copy(others, others, s_send.at[q]).wait()
        pltpu.make_async_copy(others, others, s_recv.at[q]).wait()
        own[q].wait()
    x_out.wait()


def on_device(grad_x, grad_y, coherence, pairs):
    f32 = jnp.float32
    dma = pltpu.SemaphoreType.DMA
    halo = pltpu.VMEM((K, ROWS + 16, COLS), f32)
    return pl.pallas_call(
        kernel,
        out_shape=(
            jax.ShapeDtypeStruct((K, ROWS, COLS), f32),
            jax.ShapeDtypeStruct((OWN, ROWS, COLS), f32),
        ),
        in_specs=[pl.BlockSpec(memory_space=pl.ANY)] * 3 + [pl.BlockSpec(memory_space=pltpu.VMEM)],
        out_specs=(pl.BlockSpec(memory_space=pl.ANY),) * 2,
        scratch_shapes=[
            pltpu.VMEM((K, ROWS, COLS), f32),
            halo, halo, halo, halo, halo, halo, halo,
            pltpu.VMEM((K, ROWS, COLS), f32),
            pltpu.VMEM((K, 6, 8, 128), f32),
            pltpu.VMEM((STRIPS, 6 * K, 128), f32),
            pltpu.VMEM((6 * K, 128), f32),
            pltpu.VMEM((3, K, 128), f32),
            pltpu.VMEM((IFGS, DATES, 128), f32),
            pltpu.VMEM((IFGS, 32, 128), f32),
            pltpu.VMEM((DATES, 32, 128), f32),
            dma((K, 3)), dma((5,)), dma((5,)), dma, dma,
            dma((CHUNKS,)), dma((CHUNKS,)), dma((CHUNKS,)), dma((CHUNKS,)), dma((CHUNKS + 1,)),
        ],
        compiler_params=pltpu.CompilerParams(
            collective_id=0, has_side_effects=True, vmem_limit_bytes=48 * 1024 * 1024
        ),
    )(grad_x, grad_y, coherence, pairs)


def solution(mesh):
    split = P("ifg", "strip", None)
    return jax.shard_map(
        on_device, mesh=mesh, in_specs=(split, split, split, P()), out_specs=(split, split),
        check_vma=False,
    )
```

time: 324 us -> 65.3 us (0.20)
  blocking collectives: 152 us -> 0 us
  starting transfers between devices: 75.1 us -> 0 us
  Pallas kernels: 0 us -> 58.3 us
  waiting for transfers between devices: 39.1 us -> 0 us
  other arithmetic: 33.5 us -> 0 us
  local copies, waits for them, and re-layouts: 20.2 us -> 6.21 us
    psum x5 -> x0, blocking collectives: 152 us -> none  [the longest x3 91.3 us: squares(): return lax.psum(jnp.sum(residual * residual, axis=(1, 2)), 'strip')]
    pallas_call x0 -> x1, Pallas kernels: none -> 58.3 us  [on_device(): pl.pallas_call(kernel, out_shape=(jax.ShapeDtypeStruct((K, ROWS, COLS), f...]
    all_to_all x2 -> x0, starting transfers between devices: 53 us -> none  [the longest x1 49.5 us: on_device(): lax.all_to_all(solution, 'ifg', split_axis=2, concat_axis=0, tiled=True)]
    all_to_all x2 -> x0, waiting for transfers between devices: 36.1 us -> none  [the longest x1 20.4 us: on_device(): lax.all_to_all(solution, 'ifg', split_axis=2, concat_axis=0, tiled=True)]
    ppermute x8 -> x0, starting transfers between devices: 22.1 us -> none  [the longest x4 16.8 us: extended(): before = lax.ppermute(last, axis, up)]
    reduce_sum x5 -> x0, other arithmetic: 8.21 us -> none  [the longest x3 4.58 us: on_device(): curve = lax.psum(jnp.sum(direction * image, axis=(1, 2)), 'strip')]
    another operation x5 -> x0, other arithmetic: 6.68 us -> none  [the longest x3 3.6 us: inverse_map(): factor = jnp.linalg.cholesky(normal)]
    add x3 -> x0, other arithmetic: 5.74 us -> none  [the longest x2 4.01 us: on_device(): direction = residual + (norm_next / norm_now)[:, None, None] * direction]
  transfers between devices with their start and end apart: 10 -> 0, of which waited for: 6 -> 0; matrix products, arithmetic and copies ran while one was open for 4% -> 0% of each run, Pallas kernels for 0% -> 0%
where the time goes in v1:
time: 65.3 us; the launch traced here: 65.1 us
  Pallas kernels  58.3 us (89%)
  local copies, waits for them, and re-layouts  6.21 us (10%)
    pallas_call x1, Pallas kernels, on_device(): pl.pallas_call(kernel, out_shape=(jax.ShapeDtypeStruct((K, ROWS, COLS), f...  58.3 us
    unnamed x9, local copies, waits for them, and re-layouts  6.21 us

profile of v1, /device:TPU:1, one launch (start us, length us, event | category | flops | bytes accessed | tf_op | source)
XLA Modules:
  0.0 65.1 jit_solution(17490298511068316850)
XLA Ops:
  0.6 0.8 %copy.6.pairs_ref = s32[64,2]{1,0:T(8,128)S(1)} copy(s32[64,2]{0,1:T(2,128)} %param.7) | data formatting | bytes 1024 | tf_op args[3]
  1.4 0.0 copy-start
  1.4 1.2 %copy-done = f32[4,64,1024]{2,1,0:T(8,128)S(1)} copy-done((f32[4,64,1024]{2,1,0:T(8,128)S(1)}, f32[4,64,1024]{2,1,0:T(8,128)}, u32[]{:S(2)}) %copy-start) | copy-done | bytes 1048600
  2.6 0.0 copy-start.1
  2.6 1.2 %copy-done.1 = f32[4,64,1024]{2,1,0:T(8,128)S(1)} copy-done((f32[4,64,1024]{2,1,0:T(8,128)S(1)}, f32[4,64,1024]{2,1,0:T(8,128)}, u32[]{:S(2)}) %copy-start.1) | copy-done | bytes 1048600
  3.8 0.0 copy-start.2
  3.9 1.2 %copy-done.2 = f32[4,64,1024]{2,1,0:T(8,128)S(1)} copy-done((f32[4,64,1024]{2,1,0:T(8,128)S(1)}, f32[4,64,1024]{2,1,0:T(8,128)}, u32[]{:S(2)}) %copy-start.2) | copy-done | bytes 1048600
  5.1 58.3 %shard_map.59 = (f32[4,64,1024]{2,1,0:T(8,128)S(1)}, f32[2,64,1024]{2,1,0:T(8,128)S(1)}) custom-call(f32[4,64,1024]{2,1,0:T(8,128)S(1)} %copy-done, f32[4,64,1024]{2,1,0:T(8,128)S(1)} %copy-done.1, f32[4,64,1024]{2,1,0:T(8,128)S(1)} %copy-done.2, s32[64,2]{1,0:T(8,128)S(1)} %copy.6.pairs_ref), custom_call_target="tpu_custom_call" | custom-call | tf_op jit(solution)/shard_map/pallas_call | solution.py:399
  63.4 1.0 %copy.9 = f32[4,64,1024]{2,1,0:T(8,128)} copy(f32[4,64,1024]{2,1,0:T(8,128)S(1)} %get-tuple-element.4) | data formatting | bytes 2097152
  64.3 0.8 %copy.10 = f32[2,64,1024]{2,1,0:T(8,128)} copy(f32[2,64,1024]{2,1,0:T(8,128)S(1)} %get-tuple-element.5) | data formatting | bytes 1048576
Async XLA Ops:
  1.4 1.2 %copy-start = (f32[4,64,1024]{2,1,0:T(8,128)S(1)}, f32[4,64,1024]{2,1,0:T(8,128)}, u32[]{:S(2)}) copy-start(f32[4,64,1024]{2,1,0:T(8,128)} %gx_hbm.1) | copy-start | bytes 3145732
  2.6 1.2 %copy-start.1 = (f32[4,64,1024]{2,1,0:T(8,128)S(1)}, f32[4,64,1024]{2,1,0:T(8,128)}, u32[]{:S(2)}) copy-start(f32[4,64,1024]{2,1,0:T(8,128)} %gy_hbm.1) | copy-start | bytes 3145732
  3.8 1.2 %copy-start.2 = (f32[4,64,1024]{2,1,0:T(8,128)S(1)}, f32[4,64,1024]{2,1,0:T(8,128)}, u32[]{:S(2)}) copy-start(f32[4,64,1024]{2,1,0:T(8,128)} %co_hbm.1) | copy-start | bytes 3145732

commit v2 on v1

--- a/solution.py
+++ b/solution.py
@@ -100,16 +100,17 @@
 
 
 def inverse_rows(pairs):
+    date = lax.broadcasted_iota(jnp.int32, (128, IFGS), 0)
+    design = (pairs[1:2, :] == date).astype(jnp.float32) - (pairs[0:1, :] == date).astype(jnp.float32)
     lanes = lax.broadcasted_iota(jnp.int32, (IFGS, 128), 1)
-    rows = lax.broadcasted_iota(jnp.int32, (IFGS, 128), 0)
-    design = (pairs[:, 1:2] == lanes).astype(jnp.float32) - (pairs[:, 0:1] == lanes).astype(
-        jnp.float32
+    shifted = lanes - DATES == lax.broadcasted_iota(jnp.int32, (IFGS, 128), 0)
+    table = lax.dot_general(
+        design[:DATES], design, (((1,), (1,)), ((), ())), precision=lax.Precision.HIGHEST,
+        preferred_element_type=jnp.float32,
+    ) + jnp.dot(
+        design[:DATES], shifted.astype(jnp.float32), precision=lax.Precision.HIGHEST,
+        preferred_element_type=jnp.float32,
     )
-    both = design + (lanes - DATES == rows).astype(jnp.float32)
-    table = lax.dot_general(
-        design, both, (((0,), (0,)), ((), ())), precision=lax.Precision.HIGHEST,
-        preferred_element_type=jnp.float32,
-    )[:DATES]
     spread = lax.broadcasted_iota(jnp.int32, (DATES, 128), 1)
     level = lax.broadcasted_iota(jnp.int32, (DATES, 1), 0)
     table = table + (spread < DATES).astype(jnp.float32)
@@ -121,8 +122,8 @@
 
 
 def kernel(
-    gx_hbm, gy_hbm, co_hbm, pairs_ref, x_hbm, series_hbm,
-    gx, gy, co, wx, wy, v0, v1, v2, x, sums, moments, folded, coef, spread, phases, dates,
+    gx_hbm, gy_hbm, co_hbm, pairs_hbm, x_hbm, series_hbm,
+    gx, gy, co, wx, wy, v0, v1, v2, x, sums, moments, folded, coef, spread, phases, dates, pairs,
     load_sem, halo_send, halo_recv, sum_send, sum_recv, x_send, x_recv, s_send, s_recv, out_sem,
 ):
     g, s = lax.axis_index("ifg"), lax.axis_index("strip")
@@ -137,6 +138,8 @@
             )
     for copy in loads:
         copy.start()
+    pairs_in = pltpu.make_async_copy(pairs_hbm, pairs, out_sem.at[CHUNKS + 1])
+    pairs_in.start()
 
     barrier = pltpu.get_barrier_semaphore()
 
@@ -296,10 +299,6 @@
     def _(d):
         share(d).start()
 
-    table = inverse_rows(pairs_ref[...])
-    for k in range(IFGS):
-        spread[k] = jnp.broadcast_to(table[:, DATES + k : DATES + k + 1], (DATES, 128))
-
     others = moments.at[0 : STRIPS - 1]
     pltpu.make_async_copy(others, others, sum_recv).wait()
     total = moments[0]
@@ -344,6 +343,11 @@
     x_out = pltpu.make_async_copy(x, x_hbm, out_sem.at[CHUNKS])
     x_out.start()
 
+    pairs_in.wait()
+    table = inverse_rows(pairs[...])
+    for k in range(IFGS):
+        spread[k] = jnp.broadcast_to(table[:, DATES + k : DATES + k + 1], (DATES, 128))
+
     def place(q):
         row = pl.multiple_of(32 * core + 8 * q, 8)
         return series_hbm.at[:, pl.ds(row, 8), pl.ds(own_column, 128)]
@@ -392,17 +396,28 @@
     x_out.wait()
 
 
+def hand_over(x_ref, series_ref, x_out, series_out, sem):
+    copies = [pltpu.make_async_copy(x_ref.at[i], x_out.at[i], sem.at[i]) for i in range(K)]
+    copies += [
+        pltpu.make_async_copy(series_ref.at[i], series_out.at[i], sem.at[K + i]) for i in range(OWN)
+    ]
+    for copy in copies:
+        copy.start()
+    for copy in copies:
+        copy.wait()
+
+
 def on_device(grad_x, grad_y, coherence, pairs):
     f32 = jnp.float32
     dma = pltpu.SemaphoreType.DMA
     halo = pltpu.VMEM((K, ROWS + 16, COLS), f32)
-    return pl.pallas_call(
+    phases, series = pl.pallas_call(
         kernel,
         out_shape=(
             jax.ShapeDtypeStruct((K, ROWS, COLS), f32),
             jax.ShapeDtypeStruct((OWN, ROWS, COLS), f32),
         ),
-        in_specs=[pl.BlockSpec(memory_space=pl.ANY)] * 3 + [pl.BlockSpec(memory_space=pltpu.VMEM)],
+        in_specs=[pl.BlockSpec(memory_space=pl.ANY)] * 4,
         out_specs=(pl.BlockSpec(memory_space=pl.ANY),) * 2,
         scratch_shapes=[
             pltpu.VMEM((K, ROWS, COLS), f32),
@@ -415,13 +430,25 @@
             pltpu.VMEM((IFGS, DATES, 128), f32),
             pltpu.VMEM((IFGS, 32, 128), f32),
             pltpu.VMEM((DATES, 32, 128), f32),
+            pltpu.VMEM((2, IFGS), jnp.int32),
             dma((K, 3)), dma((5,)), dma((5,)), dma, dma,
-            dma((CHUNKS,)), dma((CHUNKS,)), dma((CHUNKS,)), dma((CHUNKS,)), dma((CHUNKS + 1,)),
+            dma((CHUNKS,)), dma((CHUNKS,)), dma((CHUNKS,)), dma((CHUNKS,)), dma((CHUNKS + 2,)),
         ],
         compiler_params=pltpu.CompilerParams(
-            collective_id=0, has_side_effects=True, vmem_limit_bytes=48 * 1024 * 1024
+            collective_id=0, has_side_effects=True, vmem_limit_bytes=52 * 1024 * 1024
         ),
-    )(grad_x, grad_y, coherence, pairs)
+    )(grad_x, grad_y, coherence, pairs.T)
+    return pl.pallas_call(
+        hand_over,
+        out_shape=(
+            jax.ShapeDtypeStruct((K, ROWS, COLS), f32),
+            jax.ShapeDtypeStruct((OWN, ROWS, COLS), f32),
+        ),
+        in_specs=[pl.BlockSpec(memory_space=pltpu.VMEM)] * 2,
+        out_specs=(pl.BlockSpec(memory_space=pl.ANY),) * 2,
+        scratch_shapes=[dma((K + OWN,))],
+        compiler_params=pltpu.CompilerParams(vmem_limit_bytes=4 * 1024 * 1024),
+    )(phases, series)
 
 
 def solution(mesh):

time: 65.3 us -> 60.5 us (0.926)
  local copies, waits for them, and re-layouts: 6.21 us -> 0.67 us
  Pallas kernels: 58.3 us -> 59.1 us
    unnamed x9 -> x2, local copies, waits for them, and re-layouts: 6.21 us -> 0.67 us
    pallas_call x0 -> x1, Pallas kernels: none -> 1.19 us  [on_device(): pl.pallas_call(hand_over, out_shape=(jax.ShapeDtypeStruct((K, ROWS, COLS)...]
where the time goes in v2:
time: 60.5 us; the launch traced here: 60.4 us
  Pallas kernels  59.1 us (98%)
  local copies, waits for them, and re-layouts  0.67 us (1%)
  between operations  0.65 us (1%)
    pallas_call x1, Pallas kernels, on_device(): pl.pallas_call(kernel, out_shape=(jax.ShapeDtypeStruct((K, ROWS, COLS), f...  57.9 us

profile of v2, /device:TPU:1, one launch (start us, length us, event | category | flops | bytes accessed | tf_op | source)
XLA Modules:
  0.0 60.4 jit_solution(9540677934574746501)
XLA Ops:
  0.6 0.0 copy-start
  0.6 0.7 %copy-done = s32[64,2]{0,1:T(2,128)S(1)} copy-done((s32[64,2]{0,1:T(2,128)S(1)}, s32[64,2]{0,1:T(2,128)}, u32[]{:S(2)}) %copy-start) | copy-done | bytes 536
  1.3 57.9 %shard_map.59 = (f32[4,64,1024]{2,1,0:T(8,128)S(1)}, f32[2,64,1024]{2,1,0:T(8,128)S(1)}) custom-call(f32[4,64,1024]{2,1,0:T(8,128)} %gx_hbm.1, f32[4,64,1024]{2,1,0:T(8,128)} %gy_hbm.1, f32[4,64,1024]{2,1,0:T(8,128)} %co_hbm.1, s32[2,64]{1,0:T(2,128)S(1)} %bitcast.1), custom_call_target="tpu_custom_call" | custom-call | tf_op jit(solution)/shard_map/pallas_call | solution.py:414
  59.2 1.2 %shard_map.60 = (f32[4,64,1024]{2,1,0:T(8,128)}, f32[2,64,1024]{2,1,0:T(8,128)}) custom-call(f32[4,64,1024]{2,1,0:T(8,128)S(1)} %get-tuple-element.4.x_ref, f32[2,64,1024]{2,1,0:T(8,128)S(1)} %get-tuple-element.5.series_ref), custom_call_target="tpu_custom_call" | custom-call | tf_op jit(solution)/shard_map/pallas_call | solution.py:441
Async XLA Ops:
  0.6 0.7 %copy-start = (s32[64,2]{0,1:T(2,128)S(1)}, s32[64,2]{0,1:T(2,128)}, u32[]{:S(2)}) copy-start(s32[64,2]{0,1:T(2,128)} %param.7) | copy-start | bytes 1540

commit v3 on v2

--- a/solution.py
+++ b/solution.py
@@ -12,12 +12,14 @@
 GROUPS = 16
 STRIPS = 16
 K = 4
+PAIR = 2
 OWN = 2
 ROWS = 64
 COLS = 1024
 TILES = ROWS // 8
 CHUNKS = 4
 EPS = 3e-7
+PEERS = [(dz, other) for dz in (4, 3, 5, 2, 6, 1, 7) for other in (0, 1)] + [(0, 1)]
 
 
 def tile(t):
@@ -123,22 +125,27 @@
 
 def kernel(
     gx_hbm, gy_hbm, co_hbm, pairs_hbm, x_hbm, series_hbm,
-    gx, gy, co, wx, wy, v0, v1, v2, x, sums, moments, folded, coef, spread, phases, dates, pairs,
-    load_sem, halo_send, halo_recv, sum_send, sum_recv, x_send, x_recv, s_send, s_recv, out_sem,
+    gx, gy, co, wx, wy, basis, x, sums, moments, coef, spread, phases, early, factors, dates, pairs,
+    load_sem, halo_send, halo_recv, sum_send, sum_recv, early_send, early_recv, c_send, c_recv,
+    x_send, x_recv, s_send, s_recv, x_out, own_out, pairs_sem,
 ):
     g, s = lax.axis_index("ifg"), lax.axis_index("strip")
     z, core = g // 2, lax.rem(g, 2)
     rows = rows_iota()
-
-    loads = []
-    for i in range(K):
-        for a, (src, dst, low) in enumerate(((co_hbm, co, 8), (gy_hbm, gy, 8), (gx_hbm, gx, 0))):
-            loads.append(
-                pltpu.make_async_copy(src.at[i], dst.at[i, low : low + ROWS], load_sem.at[i, a])
-            )
-    for copy in loads:
-        copy.start()
-    pairs_in = pltpu.make_async_copy(pairs_hbm, pairs, out_sem.at[CHUNKS + 1])
+    lane = lax.broadcasted_iota(jnp.int32, (1, 128), 1)
+    v0, v1, v2 = (basis.at[j] for j in range(3))
+
+    def load(n, a):
+        src, dst, low = ((co_hbm, co, 8), (gy_hbm, gy, 8), (gx_hbm, gx, 0))[a]
+        first, last = ((0, 16), (48, 64), (16, 48))[n]
+        return pltpu.make_async_copy(
+            src.at[:, first:last], dst.at[:, low + first : low + last], load_sem.at[n, a]
+        )
+
+    for n in range(3):
+        for a in range(3):
+            load(n, a).start()
+    pairs_in = pltpu.make_async_copy(pairs_hbm, pairs, pairs_sem)
     pairs_in.start()
 
     barrier = pltpu.get_barrier_semaphore()
@@ -165,14 +172,14 @@
         co[:, tile(TILES + 1), :] = nothing
         v0[:, tile(TILES + 1), :] = nothing
 
-    for copy in loads:
-        copy.wait()
-
-    @pl.loop(0, K)
-    def _(i):
-        carry = jnp.zeros((8, COLS), jnp.float32)
-        now = co[i, tile(1), :]
-        for t in range(1, TILES + 1):
+    def right_side(i, first, last):
+        now = co[i, tile(first), :]
+        if first > 1:
+            before = co[i, tile(first - 1), :]
+            carry = pltpu.roll(before * next_row(before, now) * gy[i, tile(first - 1), :], 1, 0)
+        else:
+            carry = jnp.zeros((8, COLS), jnp.float32)
+        for t in range(first, last + 1):
             after = co[i, tile(t + 1), :] if t < TILES else jnp.zeros((8, COLS), jnp.float32)
             weight_x = edge_x(now)
             weight_y = now * next_row(now, after)
@@ -187,36 +194,51 @@
             carry = turned
             now = after
 
+    for n in range(2):
+        for a in range(3):
+            load(n, a).wait()
+
+    @pl.loop(0, K)
+    def _(i):
+        right_side(i, 1, 1)
+        right_side(i, TILES, TILES)
+
     pl.semaphore_wait(barrier, STRIPS + GROUPS - 2)
 
-    def halo(n, src, dst, low, high, shift, device):
+    up = jnp.maximum(s - 1, 0)
+    down = jnp.minimum(s + 1, STRIPS - 1)
+
+    def halo(i, n, src, low, high, shift, device):
         return pltpu.make_async_remote_copy(
-            src_ref=src.at[:, low:high],
-            dst_ref=dst.at[:, low + shift : high + shift],
-            send_sem=halo_send.at[n],
-            recv_sem=halo_recv.at[n],
+            src_ref=src.at[PAIR * i : PAIR * i + PAIR, low:high],
+            dst_ref=src.at[PAIR * i : PAIR * i + PAIR, low + shift : high + shift],
+            send_sem=halo_send.at[i, n],
+            recv_sem=halo_recv.at[i, n],
             device_id=(g, device),
             device_id_type=MESH,
         )
 
-    up = jnp.maximum(s - 1, 0)
-    down = jnp.minimum(s + 1, STRIPS - 1)
-    upward = [halo(0, co, co, 8, 11, ROWS, up), halo(1, v0, v0, 8, 11, ROWS, up)]
-    downward = [
-        halo(2, co, co, 6 + ROWS, 8 + ROWS, -ROWS, down),
-        halo(3, v0, v0, 6 + ROWS, 8 + ROWS, -ROWS, down),
-        halo(4, gy, gy, 7 + ROWS, 8 + ROWS, -ROWS, down),
-    ]
-
-    @pl.when(s > 0)
-    def _():
-        for copy in upward:
-            copy.start()
-
-    @pl.when(s < STRIPS - 1)
-    def _():
-        for copy in downward:
-            copy.start()
+    def upward(i):
+        return [halo(i, 0, co, 8, 11, ROWS, up), halo(i, 1, v0, 8, 11, ROWS, up)]
+
+    def downward(i):
+        return [
+            halo(i, 2, co, 6 + ROWS, 8 + ROWS, -ROWS, down),
+            halo(i, 3, v0, 6 + ROWS, 8 + ROWS, -ROWS, down),
+            halo(i, 4, gy, 7 + ROWS, 8 + ROWS, -ROWS, down),
+        ]
+
+    for i in range(K // PAIR):
+
+        @pl.when(s > 0)
+        def _():
+            for copy in upward(i):
+                copy.start()
+
+        @pl.when(s < STRIPS - 1)
+        def _():
+            for copy in downward(i):
+                copy.start()
 
     def first_pass(i, spans):
         totals = [jnp.zeros((8, 128), jnp.float32)] * 3
@@ -242,28 +264,53 @@
             laplace(v1, v2, wx, wy, i, low, high, inner)
         return totals
 
-    @pl.loop(0, K)
-    def _(i):
+    def interior(i):
         totals = first_pass(i, [(2, 7)]) + second_pass(i, [(3, 6)])
         totals.append(energy(v2, wx, wy, i, range(3, 6)))
         for n, total in enumerate(totals):
             sums[i, n] = total
 
-    @pl.when(s > 0)
-    def _():
-        for copy in upward:
-            copy.wait_send()
-        for copy in downward:
-            copy.wait_recv()
-
-    @pl.when(s < STRIPS - 1)
-    def _():
-        for copy in downward:
-            copy.wait_send()
-        for copy in upward:
-            copy.wait_recv()
-
-    for i in range(K):
+    def target(offset):
+        dz, other = offset
+        there, half = lax.rem(z + dz, GROUPS // 2), lax.rem(core + other, 2)
+        return 2 * there + half, half, pl.multiple_of(128 * there, 128)
+
+    def send_early(d):
+        t, half, column = target(d)
+        row = pl.multiple_of(8 + 16 + 16 * half, 8)
+        return pltpu.make_async_remote_copy(
+            src_ref=basis.at[:, K - 1, pl.ds(row, 16), pl.ds(column, 128)],
+            dst_ref=early.at[g],
+            send_sem=early_send,
+            recv_sem=early_recv,
+            device_id=(t, s),
+            device_id_type=MESH,
+        )
+
+    for a in range(3):
+        load(2, a).wait()
+    right_side(K - 1, 2, TILES - 1)
+    interior(K - 1)
+
+    for offset in PEERS:
+        send_early(offset).start()
+
+    @pl.loop(0, K - 1)
+    def _(i):
+        right_side(i, 2, TILES - 1)
+        interior(i)
+
+    def share(i, d):
+        return pltpu.make_async_remote_copy(
+            src_ref=moments.at[i, s],
+            dst_ref=moments.at[i, s],
+            send_sem=sum_send.at[i],
+            recv_sem=sum_recv.at[i],
+            device_id=(g, lax.rem(s + d, STRIPS)),
+            device_id_type=MESH,
+        )
+
+    def ends(i, pair):
         low, high, beyond = co[i, tile(0), :], co[i, tile(TILES), :], co[i, tile(TILES + 1), :]
         wx[i, tile(0), :] = edge_x(low)
         wx[i, tile(TILES + 1), :] = edge_x(beyond)
@@ -277,71 +324,100 @@
             here, there = v0[i, tile(t), :], v0[i, tile(t + 1), :]
             v0[i, tile(t), :] = jnp.where(rows == 7, here - flux, here)
             v0[i, tile(t + 1), :] = jnp.where(rows == 0, there + pltpu.roll(flux, 1, 0), there)
-
-    @pl.loop(0, K)
-    def _(i):
         totals = first_pass(i, [(0, 1), (8, 9)]) + second_pass(i, [(1, 2), (7, 9)])
         totals.append(energy(v2, wx, wy, i, (1, 2, 6, 7, 8)))
+        row = jnp.zeros((1, 128), jnp.float32)
         for n, total in enumerate(totals):
-            moments[s, pl.ds(K * n + i, 1), :] = jnp.sum(sums[i, n] + total, axis=0, keepdims=True)
-
-    def share(d):
+            total = jnp.sum(sums[i, n] + total, axis=0, keepdims=True)
+            row = jnp.where(lane == n, jnp.sum(total, axis=1, keepdims=True), row)
+        moments[pair, s, pl.ds(i - PAIR * pair, 1), :] = row
+
+    for pair in range(K // PAIR):
+
+        @pl.when(s > 0)
+        def _():
+            for copy in upward(pair):
+                copy.wait_send()
+            for copy in downward(pair):
+                copy.wait_recv()
+
+        @pl.when(s < STRIPS - 1)
+        def _():
+            for copy in downward(pair):
+                copy.wait_send()
+            for copy in upward(pair):
+                copy.wait_recv()
+
+        @pl.loop(PAIR * pair, PAIR * pair + PAIR)
+        def _(i):
+            ends(i, pair)
+
+        @pl.loop(1, STRIPS)
+        def _(d):
+            share(pair, d).start()
+
+    def send_x(first, last, d, part):
+        t, half, column = target(d)
+        row = pl.multiple_of((16 + 16 * half) if part == 0 else 48 * half, 8)
         return pltpu.make_async_remote_copy(
-            src_ref=moments.at[s],
-            dst_ref=moments.at[s],
-            send_sem=sum_send,
-            recv_sem=sum_recv,
-            device_id=(g, lax.rem(s + d, STRIPS)),
-            device_id_type=MESH,
-        )
-
-    @pl.loop(1, STRIPS)
-    def _(d):
-        share(d).start()
-
-    others = moments.at[0 : STRIPS - 1]
-    pltpu.make_async_copy(others, others, sum_recv).wait()
-    total = moments[0]
-    for d in range(1, STRIPS):
-        total = total + moments[d]
-    folded[...] = jnp.broadcast_to(jnp.sum(total, axis=1, keepdims=True), folded.shape)
-    for j, c in enumerate(coefficients([folded[K * n : K * n + K, :] for n in range(6)])):
-        coef[j] = c
-
-    def send_x(d, q):
-        t = lax.rem(g + d, GROUPS)
-        row = pl.multiple_of(32 * lax.rem(t, 2) + 8 * q, 8)
-        column = pl.multiple_of(128 * (t // 2), 128)
-        return pltpu.make_async_remote_copy(
-            src_ref=x.at[:, pl.ds(row, 8), pl.ds(column, 128)],
-            dst_ref=phases.at[pl.ds(K * g, K), pl.ds(8 * q, 8)],
-            send_sem=x_send.at[q],
-            recv_sem=x_recv.at[q],
+            src_ref=x.at[first:last, pl.ds(row, 16), pl.ds(column, 128)],
+            dst_ref=phases.at[pl.ds(K * g + first, last - first), 16 * part : 16 * part + 16],
+            send_sem=x_send.at[part],
+            recv_sem=x_recv.at[part],
             device_id=(t, s),
             device_id_type=MESH,
         )
 
+    def send_c(d):
+        return pltpu.make_async_remote_copy(
+            src_ref=coef.at[K - 1],
+            dst_ref=factors.at[g],
+            send_sem=c_send,
+            recv_sem=c_recv,
+            device_id=(target(d)[0], s),
+            device_id_type=MESH,
+        )
+
     own_column = pl.multiple_of(128 * z, 128)
-    for q in range(CHUNKS):
-
-        @pl.loop(0, K)
+    own_rows = [pl.multiple_of(16 + 16 * core, 8), pl.multiple_of(48 * core, 8)]
+    for pair in range(K // PAIR):
+        others = moments.at[pair, 0 : STRIPS - 1]
+        pltpu.make_async_copy(others, others, sum_recv.at[pair]).wait()
+        total = moments[pair, 0]
+        for d in range(1, STRIPS):
+            total = total + moments[pair, d]
+        spots = [jnp.broadcast_to(total[:, n : n + 1], (PAIR, 128)) for n in range(6)]
+        weights = coefficients(spots)
+        for i in range(PAIR * pair, PAIR * pair + PAIR):
+            for j, c in enumerate(weights):
+                coef[i, j : j + 1, :] = c[i - PAIR * pair : i - PAIR * pair + 1, :]
+        if pair == K // PAIR - 1:
+            coef[K - 1, 3:8, :] = jnp.zeros((5, 128), jnp.float32)
+
+            for offset in PEERS:
+                send_c(offset).start()
+
+        @pl.loop(PAIR * pair, PAIR * pair + PAIR)
         def _(i):
-            c0, c1, c2 = (coef[j, pl.ds(i, 1), 0:1] for j in range(3))
-            for half in range(2):
-                t = 4 * half + q
+            c0, c1, c2 = (coef[i, j : j + 1, 0:1] for j in range(3))
+            for t in range(TILES):
                 x[i, tile(t), :] = (
-                    c0 * v0[i, tile(t + 1), :] + c1 * v1[i, tile(t + 1), :] + c2 * v2[i, tile(t + 1), :]
+                    c0 * v0[i, tile(t + 1), :]
+                    + c1 * v1[i, tile(t + 1), :]
+                    + c2 * v2[i, tile(t + 1), :]
                 )
 
-        @pl.loop(1, GROUPS)
-        def _(d):
-            send_x(d, q).start()
-
-        own_row = pl.multiple_of(32 * core + 8 * q, 8)
-        phases[pl.ds(K * g, K), tile(q), :] = x[:, pl.ds(own_row, 8), pl.ds(own_column, 128)]
-
-    x_out = pltpu.make_async_copy(x, x_hbm, out_sem.at[CHUNKS])
-    x_out.start()
+        for offset in PEERS:
+            send_x(PAIR * pair, min(PAIR * pair + PAIR, K - 1), offset, 0).start()
+
+    for offset in PEERS:
+        send_x(0, K, offset, 1).start()
+
+    pltpu.make_async_copy(x, x_hbm, x_out).start()
+    for part in range(2):
+        phases[pl.ds(K * g, K), 16 * part : 16 * part + 16, :] = x[
+            :, pl.ds(own_rows[part], 16), pl.ds(own_column, 128)
+        ]
 
     pairs_in.wait()
     table = inverse_rows(pairs[...])
@@ -349,11 +425,11 @@
         spread[k] = jnp.broadcast_to(table[:, DATES + k : DATES + k + 1], (DATES, 128))
 
     def place(q):
-        row = pl.multiple_of(32 * core + 8 * q, 8)
+        row = pl.multiple_of(own_rows[q // 2] + 8 * (q % 2), 8)
         return series_hbm.at[:, pl.ds(row, 8), pl.ds(own_column, 128)]
 
     def send_s(d, q):
-        t = lax.rem(g + d, GROUPS)
+        t = target(d)[0]
         return pltpu.make_async_remote_copy(
             src_ref=dates.at[pl.ds(OWN * t, OWN), tile(q)],
             dst_ref=place(q),
@@ -363,10 +439,27 @@
             device_id_type=MESH,
         )
 
-    own = []
+    def own_s(q):
+        return pltpu.make_async_copy(
+            dates.at[pl.ds(OWN * g, OWN), tile(q)], place(q), own_out.at[q]
+        )
+
+    middle = phases.at[0 : (K - 1) * (GROUPS - 1), 0:16]
+    outer = phases.at[0 : K * (GROUPS - 1), 16:32]
+    pltpu.make_async_copy(early.at[0 : GROUPS - 1], early.at[0 : GROUPS - 1], early_recv).wait()
+    pltpu.make_async_copy(factors.at[0 : GROUPS - 1], factors.at[0 : GROUPS - 1], c_recv).wait()
+
+    @pl.loop(1, GROUPS)
+    def _(d):
+        t = lax.rem(g + d, GROUPS)
+        c0, c1, c2 = (factors[t, j : j + 1, :] for j in range(3))
+        phases[K * t + K - 1, 0:16, :] = c0 * early[t, 0] + c1 * early[t, 1] + c2 * early[t, 2]
+
     for q in range(CHUNKS):
-        others = phases.at[0 : K * (GROUPS - 1), tile(q)]
-        pltpu.make_async_copy(others, others, x_recv.at[q]).wait()
+        if q == 0:
+            pltpu.make_async_copy(middle, middle, x_recv.at[0]).wait()
+        if q == 2:
+            pltpu.make_async_copy(outer, outer, x_recv.at[1]).wait()
 
         def add(k, totals):
             phase = phases[k, tile(q), :]
@@ -378,22 +471,24 @@
         for d in range(DATES):
             dates[d, tile(q), :] = totals[d]
 
-        @pl.loop(1, GROUPS)
-        def _(d):
-            send_s(d, q).start()
-
-        own.append(pltpu.make_async_copy(dates.at[pl.ds(OWN * g, OWN), tile(q)], place(q), out_sem.at[q]))
-        own[q].start()
-
-    pltpu.make_async_copy(moments.at[0 : STRIPS - 1], moments.at[0 : STRIPS - 1], sum_send).wait()
+        for offset in PEERS:
+            send_s(offset, q).start()
+
+        own_s(q).start()
+
+    for pair in range(K // PAIR):
+        others = moments.at[pair, 0 : STRIPS - 1]
+        pltpu.make_async_copy(others, others, sum_send.at[pair]).wait()
+    pltpu.make_async_copy(x, x_hbm, x_out).wait()
+    pltpu.make_async_copy(early.at[0 : GROUPS - 1], early.at[0 : GROUPS - 1], early_send).wait()
+    pltpu.make_async_copy(factors.at[0 : GROUPS - 1], factors.at[0 : GROUPS - 1], c_send).wait()
+    pltpu.make_async_copy(middle, middle, x_send.at[0]).wait()
+    pltpu.make_async_copy(outer, outer, x_send.at[1]).wait()
     for q in range(CHUNKS):
-        others = phases.at[0 : K * (GROUPS - 1), tile(q)]
-        pltpu.make_async_copy(others, others, x_send.at[q]).wait()
         others = dates.at[0 : OWN * (GROUPS - 1), tile(q)]
         pltpu.make_async_copy(others, others, s_send.at[q]).wait()
         pltpu.make_async_copy(others, others, s_recv.at[q]).wait()
-        own[q].wait()
-    x_out.wait()
+        own_s(q).wait()
 
 
 def hand_over(x_ref, series_ref, x_out, series_out, sem):
@@ -417,22 +512,25 @@
             jax.ShapeDtypeStruct((K, ROWS, COLS), f32),
             jax.ShapeDtypeStruct((OWN, ROWS, COLS), f32),
         ),
-        in_specs=[pl.BlockSpec(memory_space=pl.ANY)] * 4,
+        in_specs=[pl.BlockSpec(memory_space=pltpu.HBM)] * 4,
         out_specs=(pl.BlockSpec(memory_space=pl.ANY),) * 2,
         scratch_shapes=[
             pltpu.VMEM((K, ROWS, COLS), f32),
-            halo, halo, halo, halo, halo, halo, halo,
+            halo, halo, halo, halo,
+            pltpu.VMEM((3, K, ROWS + 16, COLS), f32),
             pltpu.VMEM((K, ROWS, COLS), f32),
             pltpu.VMEM((K, 6, 8, 128), f32),
-            pltpu.VMEM((STRIPS, 6 * K, 128), f32),
-            pltpu.VMEM((6 * K, 128), f32),
-            pltpu.VMEM((3, K, 128), f32),
+            pltpu.VMEM((K // PAIR, STRIPS, PAIR, 128), f32),
+            pltpu.VMEM((K, 8, 128), f32),
             pltpu.VMEM((IFGS, DATES, 128), f32),
             pltpu.VMEM((IFGS, 32, 128), f32),
+            pltpu.VMEM((GROUPS, 3, 16, 128), f32),
+            pltpu.VMEM((GROUPS, 8, 128), f32),
             pltpu.VMEM((DATES, 32, 128), f32),
             pltpu.VMEM((2, IFGS), jnp.int32),
-            dma((K, 3)), dma((5,)), dma((5,)), dma, dma,
-            dma((CHUNKS,)), dma((CHUNKS,)), dma((CHUNKS,)), dma((CHUNKS,)), dma((CHUNKS + 2,)),
+            dma((3, 3)), dma((K // PAIR, 5)), dma((K // PAIR, 5)), dma((K // PAIR,)), dma((K // PAIR,)),
+            dma, dma, dma, dma,
+            dma((2,)), dma((2,)), dma((CHUNKS,)), dma((CHUNKS,)), dma, dma((CHUNKS,)), dma,
         ],
         compiler_params=pltpu.CompilerParams(
             collective_id=0, has_side_effects=True, vmem_limit_bytes=52 * 1024 * 1024

time: 60.5 us -> 57.7 us (0.954)
  Pallas kernels: 59.1 us -> 56.2 us
    pallas_call x1, Pallas kernels: 57.9 us -> 55.1 us  [on_device(): pl.pallas_call(kernel, out_shape=(jax.ShapeDtypeStruct((K, ROWS, COLS), f...]
where the time goes in v3:
time: 57.7 us; the launch traced here: 57.6 us
  Pallas kernels  56.2 us (97%)
  local copies, waits for them, and re-layouts  0.67 us (1%)
  between operations  0.65 us (1%)
    pallas_call x1, Pallas kernels, on_device(): pl.pallas_call(kernel, out_shape=(jax.ShapeDtypeStruct((K, ROWS, COLS), f...  55.1 us
    pallas_call x1, Pallas kernels, on_device(): pl.pallas_call(hand_over, out_shape=(jax.ShapeDtypeStruct((K, ROWS, COLS)...  1.19 us

profile of v3, /device:TPU:1, one launch (start us, length us, event | category | flops | bytes accessed | tf_op | source)
XLA Modules:
  0.0 57.6 jit_solution(4182730847769449120)
XLA Ops:
  0.6 0.0 copy-start
  0.6 0.7 %copy-done = s32[64,2]{0,1:T(2,128)S(1)} copy-done((s32[64,2]{0,1:T(2,128)S(1)}, s32[64,2]{0,1:T(2,128)}, u32[]{:S(2)}) %copy-start) | copy-done | bytes 536
  1.3 55.1 %shard_map.59 = (f32[4,64,1024]{2,1,0:T(8,128)S(1)}, f32[2,64,1024]{2,1,0:T(8,128)S(1)}) custom-call(f32[4,64,1024]{2,1,0:T(8,128)} %gx_hbm.1, f32[4,64,1024]{2,1,0:T(8,128)} %gy_hbm.1, f32[4,64,1024]{2,1,0:T(8,128)} %co_hbm.1, s32[2,64]{1,0:T(2,128)S(1)} %bitcast.1), custom_call_target="tpu_custom_call" | custom-call | tf_op jit(solution)/shard_map/pallas_call | solution.py:509
  56.4 1.2 %shard_map.60 = (f32[4,64,1024]{2,1,0:T(8,128)}, f32[2,64,1024]{2,1,0:T(8,128)}) custom-call(f32[4,64,1024]{2,1,0:T(8,128)S(1)} %get-tuple-element.4.x_ref, f32[2,64,1024]{2,1,0:T(8,128)S(1)} %get-tuple-element.5.series_ref), custom_call_target="tpu_custom_call" | custom-call | tf_op jit(solution)/shard_map/pallas_call | solution.py:539
Async XLA Ops:
  0.6 0.7 %copy-start = (s32[64,2]{0,1:T(2,128)S(1)}, s32[64,2]{0,1:T(2,128)}, u32[]{:S(2)}) copy-start(s32[64,2]{0,1:T(2,128)} %param.7) | copy-start | bytes 1540

commit v4 on v3

--- a/solution.py
+++ b/solution.py
@@ -12,13 +12,16 @@
 GROUPS = 16
 STRIPS = 16
 K = 4
-PAIR = 2
+BATCHES = ((0, 1), (1, 2), (2, 4))
 OWN = 2
 ROWS = 64
 COLS = 1024
 TILES = ROWS // 8
 CHUNKS = 4
 EPS = 3e-7
+EARLY = (16, 8)
+OTHERS = [(dz, 1) for dz in (4, 3, 5, 2, 6, 1, 7, 0)]
+STRIP_PEERS = [(dy, dx) for dy in (2, 1, 3, 0) for dx in (2, 1, 3, 0) if (dy, dx) != (0, 0)]
 PEERS = [(dz, other) for dz in (4, 3, 5, 2, 6, 1, 7) for other in (0, 1)] + [(0, 1)]
 
 
@@ -150,14 +153,18 @@
 
     barrier = pltpu.get_barrier_semaphore()
 
-    @pl.loop(1, STRIPS)
-    def _(d):
-        pl.semaphore_signal(
-            barrier, inc=1, device_id=(g, lax.rem(s + d, STRIPS)), device_id_type=MESH
-        )
-        pl.semaphore_signal(
-            barrier, inc=1, device_id=(lax.rem(g + d, GROUPS), s), device_id_type=MESH
-        )
+    def beside(offset):
+        dy, dx = offset
+        return g, 4 * lax.rem(s // 4 + dy, 4) + lax.rem(lax.rem(s, 4) + dx, 4)
+
+    def behind(offset):
+        dz, other = offset
+        return 2 * lax.rem(z + dz, GROUPS // 2) + lax.rem(core + other, 2), s
+
+    for offset in PEERS:
+        pl.semaphore_signal(barrier, inc=1, device_id=behind(offset), device_id_type=MESH)
+    for offset in STRIP_PEERS:
+        pl.semaphore_signal(barrier, inc=1, device_id=beside(offset), device_id_type=MESH)
 
     nothing = jnp.zeros((K, 8, COLS), jnp.float32)
 
@@ -210,8 +217,8 @@
 
     def halo(i, n, src, low, high, shift, device):
         return pltpu.make_async_remote_copy(
-            src_ref=src.at[PAIR * i : PAIR * i + PAIR, low:high],
-            dst_ref=src.at[PAIR * i : PAIR * i + PAIR, low + shift : high + shift],
+            src_ref=src.at[slice(*BATCHES[i]), low:high],
+            dst_ref=src.at[slice(*BATCHES[i]), low + shift : high + shift],
             send_sem=halo_send.at[i, n],
             recv_sem=halo_recv.at[i, n],
             device_id=(g, device),
@@ -228,7 +235,7 @@
             halo(i, 4, gy, 7 + ROWS, 8 + ROWS, -ROWS, down),
         ]
 
-    for i in range(K // PAIR):
+    for i in range(len(BATCHES)):
 
         @pl.when(s > 0)
         def _():
@@ -279,10 +286,10 @@
         t, half, column = target(d)
         row = pl.multiple_of(8 + 16 + 16 * half, 8)
         return pltpu.make_async_remote_copy(
-            src_ref=basis.at[:, K - 1, pl.ds(row, 16), pl.ds(column, 128)],
-            dst_ref=early.at[g],
-            send_sem=early_send,
-            recv_sem=early_recv,
+            src_ref=basis.at[:, K - 1, pl.ds(row, EARLY[offset[1]]), pl.ds(column, 128)],
+            dst_ref=early.at[g, :, 0 : EARLY[offset[1]]],
+            send_sem=early_send.at[offset[1]],
+            recv_sem=early_recv.at[offset[1]],
             device_id=(t, s),
             device_id_type=MESH,
         )
@@ -295,22 +302,17 @@
     for offset in PEERS:
         send_early(offset).start()
 
-    @pl.loop(0, K - 1)
-    def _(i):
-        right_side(i, 2, TILES - 1)
-        interior(i)
-
-    def share(i, d):
+    def share(i, offset):
         return pltpu.make_async_remote_copy(
             src_ref=moments.at[i, s],
             dst_ref=moments.at[i, s],
             send_sem=sum_send.at[i],
             recv_sem=sum_recv.at[i],
-            device_id=(g, lax.rem(s + d, STRIPS)),
-            device_id_type=MESH,
-        )
-
-    def ends(i, pair):
+            device_id=beside(offset),
+            device_id_type=MESH,
+        )
+
+    def ends(i, batch):
         low, high, beyond = co[i, tile(0), :], co[i, tile(TILES), :], co[i, tile(TILES + 1), :]
         wx[i, tile(0), :] = edge_x(low)
         wx[i, tile(TILES + 1), :] = edge_x(beyond)
@@ -330,31 +332,35 @@
         for n, total in enumerate(totals):
             total = jnp.sum(sums[i, n] + total, axis=0, keepdims=True)
             row = jnp.where(lane == n, jnp.sum(total, axis=1, keepdims=True), row)
-        moments[pair, s, pl.ds(i - PAIR * pair, 1), :] = row
-
-    for pair in range(K // PAIR):
+        moments[batch, s, pl.ds(i - BATCHES[batch][0], 1), :] = row
+
+    for batch in range(len(BATCHES)):
+
+        @pl.loop(BATCHES[batch][0], min(BATCHES[batch][1], K - 1))
+        def _(i):
+            right_side(i, 2, TILES - 1)
+            interior(i)
 
         @pl.when(s > 0)
         def _():
-            for copy in upward(pair):
+            for copy in upward(batch):
                 copy.wait_send()
-            for copy in downward(pair):
+            for copy in downward(batch):
                 copy.wait_recv()
 
         @pl.when(s < STRIPS - 1)
         def _():
-            for copy in downward(pair):
+            for copy in downward(batch):
                 copy.wait_send()
-            for copy in upward(pair):
+            for copy in upward(batch):
                 copy.wait_recv()
 
-        @pl.loop(PAIR * pair, PAIR * pair + PAIR)
+        @pl.loop(*BATCHES[batch])
         def _(i):
-            ends(i, pair)
-
-        @pl.loop(1, STRIPS)
-        def _(d):
-            share(pair, d).start()
+            ends(i, batch)
+
+        for offset in STRIP_PEERS:
+            share(batch, offset).start()
 
     def send_x(first, last, d, part):
         t, half, column = target(d)
@@ -368,6 +374,18 @@
             device_id_type=MESH,
         )
 
+    def send_rest(offset):
+        t, half, column = target(offset)
+        row = pl.multiple_of(24 + 16 * half, 8)
+        return pltpu.make_async_remote_copy(
+            src_ref=x.at[K - 1 : K, pl.ds(row, 8), pl.ds(column, 128)],
+            dst_ref=phases.at[pl.ds(K * g + K - 1, 1), 8:16],
+            send_sem=x_send.at[2],
+            recv_sem=x_recv.at[2],
+            device_id=(t, s),
+            device_id_type=MESH,
+        )
+
     def send_c(d):
         return pltpu.make_async_remote_copy(
             src_ref=coef.at[K - 1],
@@ -378,38 +396,43 @@
             device_id_type=MESH,
         )
 
+    def phase(i):
+        c0, c1, c2 = (coef[i, j : j + 1, 0:1] for j in range(3))
+        for t in range(TILES):
+            x[i, tile(t), :] = (
+                c0 * v0[i, tile(t + 1), :]
+                + c1 * v1[i, tile(t + 1), :]
+                + c2 * v2[i, tile(t + 1), :]
+            )
+
     own_column = pl.multiple_of(128 * z, 128)
     own_rows = [pl.multiple_of(16 + 16 * core, 8), pl.multiple_of(48 * core, 8)]
-    for pair in range(K // PAIR):
-        others = moments.at[pair, 0 : STRIPS - 1]
-        pltpu.make_async_copy(others, others, sum_recv.at[pair]).wait()
-        total = moments[pair, 0]
+    for batch in range(len(BATCHES)):
+        others = moments.at[batch, 0 : STRIPS - 1]
+        pltpu.make_async_copy(others, others, sum_recv.at[batch]).wait()
+        total = moments[batch, 0]
         for d in range(1, STRIPS):
-            total = total + moments[pair, d]
-        spots = [jnp.broadcast_to(total[:, n : n + 1], (PAIR, 128)) for n in range(6)]
+            total = total + moments[batch, d]
+        spots = [jnp.broadcast_to(total[:, n : n + 1], total.shape) for n in range(6)]
         weights = coefficients(spots)
-        for i in range(PAIR * pair, PAIR * pair + PAIR):
+        first, last = BATCHES[batch]
+        for i in range(first, last):
             for j, c in enumerate(weights):
-                coef[i, j : j + 1, :] = c[i - PAIR * pair : i - PAIR * pair + 1, :]
-        if pair == K // PAIR - 1:
-            coef[K - 1, 3:8, :] = jnp.zeros((5, 128), jnp.float32)
-
-            for offset in PEERS:
-                send_c(offset).start()
-
-        @pl.loop(PAIR * pair, PAIR * pair + PAIR)
+                coef[i, j : j + 1, :] = c[i - first : i - first + 1, :]
+
+        @pl.loop(first, min(last, K - 1))
         def _(i):
-            c0, c1, c2 = (coef[i, j : j + 1, 0:1] for j in range(3))
-            for t in range(TILES):
-                x[i, tile(t), :] = (
-                    c0 * v0[i, tile(t + 1), :]
-                    + c1 * v1[i, tile(t + 1), :]
-                    + c2 * v2[i, tile(t + 1), :]
-                )
+            phase(i)
 
         for offset in PEERS:
-            send_x(PAIR * pair, min(PAIR * pair + PAIR, K - 1), offset, 0).start()
-
+            send_x(first, min(last, K - 1), offset, 0).start()
+
+    coef[K - 1, 3:8, :] = jnp.zeros((5, 128), jnp.float32)
+    for offset in PEERS:
+        send_c(offset).start()
+    phase(K - 1)
+    for offset in OTHERS:
+        send_rest(offset).start()
     for offset in PEERS:
         send_x(0, K, offset, 1).start()
 
@@ -446,18 +469,23 @@
 
     middle = phases.at[0 : (K - 1) * (GROUPS - 1), 0:16]
     outer = phases.at[0 : K * (GROUPS - 1), 16:32]
-    pltpu.make_async_copy(early.at[0 : GROUPS - 1], early.at[0 : GROUPS - 1], early_recv).wait()
+    halves = (early.at[0 : GROUPS // 2 - 1, :, 0 : EARLY[0]], early.at[0 : GROUPS // 2, :, 0 : EARLY[1]])
+    rest = phases.at[0 : GROUPS // 2, 8:16]
+    for other in range(2):
+        pltpu.make_async_copy(halves[other], halves[other], early_recv.at[other]).wait()
     pltpu.make_async_copy(factors.at[0 : GROUPS - 1], factors.at[0 : GROUPS - 1], c_recv).wait()
 
-    @pl.loop(1, GROUPS)
-    def _(d):
-        t = lax.rem(g + d, GROUPS)
+    for offset in PEERS:
+        t, count = target(offset)[0], EARLY[offset[1]]
         c0, c1, c2 = (factors[t, j : j + 1, :] for j in range(3))
-        phases[K * t + K - 1, 0:16, :] = c0 * early[t, 0] + c1 * early[t, 1] + c2 * early[t, 2]
+        e0, e1, e2 = (early[t, j, 0:count, :] for j in range(3))
+        phases[K * t + K - 1, 0:count, :] = c0 * e0 + c1 * e1 + c2 * e2
 
     for q in range(CHUNKS):
         if q == 0:
             pltpu.make_async_copy(middle, middle, x_recv.at[0]).wait()
+        if q == 1:
+            pltpu.make_async_copy(rest, rest, x_recv.at[2]).wait()
         if q == 2:
             pltpu.make_async_copy(outer, outer, x_recv.at[1]).wait()
 
@@ -476,11 +504,13 @@
 
         own_s(q).start()
 
-    for pair in range(K // PAIR):
-        others = moments.at[pair, 0 : STRIPS - 1]
-        pltpu.make_async_copy(others, others, sum_send.at[pair]).wait()
+    for batch in range(len(BATCHES)):
+        others = moments.at[batch, 0 : STRIPS - 1]
+        pltpu.make_async_copy(others, others, sum_send.at[batch]).wait()
     pltpu.make_async_copy(x, x_hbm, x_out).wait()
-    pltpu.make_async_copy(early.at[0 : GROUPS - 1], early.at[0 : GROUPS - 1], early_send).wait()
+    for other in range(2):
+        pltpu.make_async_copy(halves[other], halves[other], early_send.at[other]).wait()
+    pltpu.make_async_copy(rest, rest, x_send.at[2]).wait()
     pltpu.make_async_copy(factors.at[0 : GROUPS - 1], factors.at[0 : GROUPS - 1], c_send).wait()
     pltpu.make_async_copy(middle, middle, x_send.at[0]).wait()
     pltpu.make_async_copy(outer, outer, x_send.at[1]).wait()
@@ -520,7 +550,7 @@
             pltpu.VMEM((3, K, ROWS + 16, COLS), f32),
             pltpu.VMEM((K, ROWS, COLS), f32),
             pltpu.VMEM((K, 6, 8, 128), f32),
-            pltpu.VMEM((K // PAIR, STRIPS, PAIR, 128), f32),
+            pltpu.VMEM((len(BATCHES), STRIPS, K, 128), f32),
             pltpu.VMEM((K, 8, 128), f32),
             pltpu.VMEM((IFGS, DATES, 128), f32),
             pltpu.VMEM((IFGS, 32, 128), f32),
@@ -528,9 +558,9 @@
             pltpu.VMEM((GROUPS, 8, 128), f32),
             pltpu.VMEM((DATES, 32, 128), f32),
             pltpu.VMEM((2, IFGS), jnp.int32),
-            dma((3, 3)), dma((K // PAIR, 5)), dma((K // PAIR, 5)), dma((K // PAIR,)), dma((K // PAIR,)),
-            dma, dma, dma, dma,
-            dma((2,)), dma((2,)), dma((CHUNKS,)), dma((CHUNKS,)), dma, dma((CHUNKS,)), dma,
+            dma((3, 3)), dma((len(BATCHES), 5)), dma((len(BATCHES), 5)), dma((len(BATCHES),)), dma((len(BATCHES),)),
+            dma((2,)), dma((2,)), dma, dma,
+            dma((3,)), dma((3,)), dma((CHUNKS,)), dma((CHUNKS,)), dma, dma((CHUNKS,)), dma,
         ],
         compiler_params=pltpu.CompilerParams(
             collective_id=0, has_side_effects=True, vmem_limit_bytes=52 * 1024 * 1024

time: 57.7 us -> 56.6 us (0.981)
  Pallas kernels: 56.2 us -> 55.2 us
    pallas_call x1, Pallas kernels: 55.1 us -> 54 us  [on_device(): pl.pallas_call(kernel, out_shape=(jax.ShapeDtypeStruct((K, ROWS, COLS), f...]
where the time goes in v4:
time: 56.6 us; the launch traced here: 56.5 us
  Pallas kernels  55.2 us (98%)
  local copies, waits for them, and re-layouts  0.67 us (1%)
  between operations  0.65 us (1%)
    pallas_call x1, Pallas kernels, on_device(): pl.pallas_call(kernel, out_shape=(jax.ShapeDtypeStruct((K, ROWS, COLS), f...  54 us
    pallas_call x1, Pallas kernels, on_device(): pl.pallas_call(hand_over, out_shape=(jax.ShapeDtypeStruct((K, ROWS, COLS)...  1.19 us

profile of v4, /device:TPU:1, one launch (start us, length us, event | category | flops | bytes accessed | tf_op | source)
XLA Modules:
  0.0 56.5 jit_solution(7830034153544796267)
XLA Ops:
  0.6 0.0 copy-start
  0.6 0.7 %copy-done = s32[64,2]{0,1:T(2,128)S(1)} copy-done((s32[64,2]{0,1:T(2,128)S(1)}, s32[64,2]{0,1:T(2,128)}, u32[]{:S(2)}) %copy-start) | copy-done | bytes 536
  1.3 54.0 %shard_map.59 = (f32[4,64,1024]{2,1,0:T(8,128)S(1)}, f32[2,64,1024]{2,1,0:T(8,128)S(1)}) custom-call(f32[4,64,1024]{2,1,0:T(8,128)} %gx_hbm.1, f32[4,64,1024]{2,1,0:T(8,128)} %gy_hbm.1, f32[4,64,1024]{2,1,0:T(8,128)} %co_hbm.1, s32[2,64]{1,0:T(2,128)S(1)} %bitcast.1), custom_call_target="tpu_custom_call" | custom-call | tf_op jit(solution)/shard_map/pallas_call | solution.py:539
  55.3 1.2 %shard_map.60 = (f32[4,64,1024]{2,1,0:T(8,128)}, f32[2,64,1024]{2,1,0:T(8,128)}) custom-call(f32[4,64,1024]{2,1,0:T(8,128)S(1)} %get-tuple-element.4.x_ref, f32[2,64,1024]{2,1,0:T(8,128)S(1)} %get-tuple-element.5.series_ref), custom_call_target="tpu_custom_call" | custom-call | tf_op jit(solution)/shard_map/pallas_call | solution.py:569
Async XLA Ops:
  0.6 0.7 %copy-start = (s32[64,2]{0,1:T(2,128)S(1)}, s32[64,2]{0,1:T(2,128)}, u32[]{:S(2)}) copy-start(s32[64,2]{0,1:T(2,128)} %param.7) | copy-start | bytes 1540

commit v5 on v4

--- a/solution.py
+++ b/solution.py
@@ -210,6 +210,58 @@
         right_side(i, 1, 1)
         right_side(i, TILES, TILES)
 
+    def first_pass(i, spans):
+        totals = [jnp.zeros((8, 128), jnp.float32)] * 3
+
+        def inner(t, p, q):
+            if 1 <= t <= TILES:
+                for n, product in enumerate((p * p, p * q, q * q)):
+                    totals[n] = totals[n] + fold(product)
+
+        for low, high in spans:
+            laplace(v0, v1, wx, wy, i, low, high, inner)
+        return totals
+
+    def second_pass(i, spans):
+        totals = [jnp.zeros((8, 128), jnp.float32)] * 2
+
+        def inner(t, p, q):
+            if 1 <= t <= TILES:
+                for n, product in enumerate((p * q, q * q)):
+                    totals[n] = totals[n] + fold(product)
+
+        for low, high in spans:
+            laplace(v1, v2, wx, wy, i, low, high, inner)
+        return totals
+
+    def interior(i):
+        totals = first_pass(i, [(2, 7)]) + second_pass(i, [(3, 6)])
+        totals.append(energy(v2, wx, wy, i, range(3, 6)))
+        for n, total in enumerate(totals):
+            sums[i, n] = total
+
+    def target(offset):
+        dz, other = offset
+        there, half = lax.rem(z + dz, GROUPS // 2), lax.rem(core + other, 2)
+        return 2 * there + half, half, pl.multiple_of(128 * there, 128)
+
+    def send_early(d):
+        t, half, column = target(d)
+        row = pl.multiple_of(8 + 16 + 16 * half, 8)
+        return pltpu.make_async_remote_copy(
+            src_ref=basis.at[:, K - 1, pl.ds(row, EARLY[offset[1]]), pl.ds(column, 128)],
+            dst_ref=early.at[g, :, 0 : EARLY[offset[1]]],
+            send_sem=early_send.at[offset[1]],
+            recv_sem=early_recv.at[offset[1]],
+            device_id=(t, s),
+            device_id_type=MESH,
+        )
+
+    for a in range(3):
+        load(2, a).wait()
+    right_side(K - 1, 2, TILES - 1)
+    interior(K - 1)
+
     pl.semaphore_wait(barrier, STRIPS + GROUPS - 2)
 
     up = jnp.maximum(s - 1, 0)
@@ -246,58 +298,6 @@
         def _():
             for copy in downward(i):
                 copy.start()
-
-    def first_pass(i, spans):
-        totals = [jnp.zeros((8, 128), jnp.float32)] * 3
-
-        def inner(t, p, q):
-            if 1 <= t <= TILES:
-                for n, product in enumerate((p * p, p * q, q * q)):
-                    totals[n] = totals[n] + fold(product)
-
-        for low, high in spans:
-            laplace(v0, v1, wx, wy, i, low, high, inner)
-        return totals
-
-    def second_pass(i, spans):
-        totals = [jnp.zeros((8, 128), jnp.float32)] * 2
-
-        def inner(t, p, q):
-            if 1 <= t <= TILES:
-                for n, product in enumerate((p * q, q * q)):
-                    totals[n] = totals[n] + fold(product)
-
-        for low, high in spans:
-            laplace(v1, v2, wx, wy, i, low, high, inner)
-        return totals
-
-    def interior(i):
-        totals = first_pass(i, [(2, 7)]) + second_pass(i, [(3, 6)])
-        totals.append(energy(v2, wx, wy, i, range(3, 6)))
-        for n, total in enumerate(totals):
-            sums[i, n] = total
-
-    def target(offset):
-        dz, other = offset
-        there, half = lax.rem(z + dz, GROUPS // 2), lax.rem(core + other, 2)
-        return 2 * there + half, half, pl.multiple_of(128 * there, 128)
-
-    def send_early(d):
-        t, half, column = target(d)
-        row = pl.multiple_of(8 + 16 + 16 * half, 8)
-        return pltpu.make_async_remote_copy(
-            src_ref=basis.at[:, K - 1, pl.ds(row, EARLY[offset[1]]), pl.ds(column, 128)],
-            dst_ref=early.at[g, :, 0 : EARLY[offset[1]]],
-            send_sem=early_send.at[offset[1]],
-            recv_sem=early_recv.at[offset[1]],
-            device_id=(t, s),
-            device_id_type=MESH,
-        )
-
-    for a in range(3):
-        load(2, a).wait()
-    right_side(K - 1, 2, TILES - 1)
-    interior(K - 1)
 
     for offset in PEERS:
         send_early(offset).start()

time: 56.6 us -> 56.8 us (level)
  no operation moved by 1% of the time
where the time goes in v5:
time: 56.8 us; the launch traced here: 56.7 us
  Pallas kernels  55.4 us (98%)
  local copies, waits for them, and re-layouts  0.67 us (1%)
  between operations  0.65 us (1%)
    pallas_call x1, Pallas kernels, on_device(): pl.pallas_call(kernel, out_shape=(jax.ShapeDtypeStruct((K, ROWS, COLS), f...  54.2 us
    pallas_call x1, Pallas kernels, on_device(): pl.pallas_call(hand_over, out_shape=(jax.ShapeDtypeStruct((K, ROWS, COLS)...  1.19 us

profile of v5, /device:TPU:1, one launch (start us, length us, event | category | flops | bytes accessed | tf_op | source)
XLA Modules:
  0.0 56.7 jit_solution(6229053367667130647)
XLA Ops:
  0.6 0.0 copy-start
  0.6 0.7 %copy-done = s32[64,2]{0,1:T(2,128)S(1)} copy-done((s32[64,2]{0,1:T(2,128)S(1)}, s32[64,2]{0,1:T(2,128)}, u32[]{:S(2)}) %copy-start) | copy-done | bytes 536
  1.3 54.2 %shard_map.59 = (f32[4,64,1024]{2,1,0:T(8,128)S(1)}, f32[2,64,1024]{2,1,0:T(8,128)S(1)}) custom-call(f32[4,64,1024]{2,1,0:T(8,128)} %gx_hbm.1, f32[4,64,1024]{2,1,0:T(8,128)} %gy_hbm.1, f32[4,64,1024]{2,1,0:T(8,128)} %co_hbm.1, s32[2,64]{1,0:T(2,128)S(1)} %bitcast.1), custom_call_target="tpu_custom_call" | custom-call | tf_op jit(solution)/shard_map/pallas_call | solution.py:539
  55.5 1.2 %shard_map.60 = (f32[4,64,1024]{2,1,0:T(8,128)}, f32[2,64,1024]{2,1,0:T(8,128)}) custom-call(f32[4,64,1024]{2,1,0:T(8,128)S(1)} %get-tuple-element.4.x_ref, f32[2,64,1024]{2,1,0:T(8,128)S(1)} %get-tuple-element.5.series_ref), custom_call_target="tpu_custom_call" | custom-call | tf_op jit(solution)/shard_map/pallas_call | solution.py:569
Async XLA Ops:
  0.6 0.7 %copy-start = (s32[64,2]{0,1:T(2,128)S(1)}, s32[64,2]{0,1:T(2,128)}, u32[]{:S(2)}) copy-start(s32[64,2]{0,1:T(2,128)} %param.7) | copy-start | bytes 1540
